TPU v7x, 32 devices: a whole 2x2x4 slice. The times are simulated.
32 devices in a mesh: dom: 32 (over z, y, x, core).
Axes of the slice: x: 2, y: 2, z: 4, core: 2. Of those that a mesh axis runs over, the one named last changes fastest.
Arguments:
- velocity: bfloat16 [3, 512, 16384], P(None, None, 'dom'), may hold values from -1.1953125 to 1.1953125
- inverse_sizes: float32 [3, 16384], P(None, 'dom'), may hold values from 0.5 to 2
- resample_x: float32 [2, 8, 8, 16384], P(None, None, None, 'dom'), may hold values from 0 to 0.25
- resample_y: float32 [2, 4, 8, 16384], P(None, None, None, 'dom'), may hold values from 0 to 0.25
- resample_z: float32 [2, 4, 8, 16384], P(None, None, None, 'dom'), may hold values from 0 to 0.25
- piece_target: int32 [2, 16384], P(None, 'dom'), may hold values from 0 to 511, as said below
- target_brick: int32 [16384, 1], P('dom'), may hold values from 0 to 31; in each aligned block of 512 rows (0 to 511, 512 to 1023, ...) at most 64 rows name the same one
- target_block: int32 [16384], P('dom'), may hold values from 0 to 2047
- brick_home: int32 [32], replicated, may hold values from 0 to 31, each once
Outputs:
- bricks: float32 [32, 2048, 128], P('dom')
Inputs may be any that keep to these rules, and one draw needn't show every extreme that they name: `piece_target`: among the 2 x 512 entries of one device's columns every value appears exactly twice. `target_brick`: in the rows of one device no brick is named more than 64 times, and in some device's rows some brick is named exactly 64 times. `brick_home`: every device is the home of exactly one brick.
All inputs are finite; a program needn't handle non-finite values.
Results may differ from a plain program's by a relative error of at most 0.0023.
Values sent between devices are 32-bit elements; how exact they have to be, the bound alone decides.
No kernel may reach another device: no remote copies, remote signals or barrier semaphores. Data moves between devices by JAX's collectives and lax.ppermute only.
A program may use at most 192 MiB of HBM per device.

v0:
```python
import math

import jax
import jax.numpy as jnp
import numpy as np
from jax import lax
from jax.sharding import PartitionSpec as P

EYN = 8
EZN = 16
BLOCKS = 2048


GLL_NODES = [
    -1.0,
    -0.8717401485096066,
    -0.5917001814331423,
    -0.2092992179024789,
    0.2092992179024789,
    0.5917001814331423,
    0.8717401485096066,
    1.0,
]


def extended(cells, sides, width):
    for axis, dim in sides:
        count = lax.axis_size(axis)
        head = lax.slice_in_dim(cells, 0, width, axis=dim)
        tail = lax.slice_in_dim(cells, cells.shape[dim] - width, cells.shape[dim], axis=dim)
        cells = jnp.concatenate(
            [
                lax.ppermute(tail, axis, [(i, (i + 1) % count) for i in range(count)]),
                cells,
                lax.ppermute(head, axis, [((i + 1) % count, i) for i in range(count)]),
            ],
            axis=dim,
        )
    return cells


def derivative_operator():
    barycentric = []
    for first in range(8):
        product_term = 1.0
        for other in range(8):
            if other != first:
                product_term = product_term * (GLL_NODES[first] - GLL_NODES[other])
        barycentric.append(1.0 / product_term)
    matrix_rows = []
    for first in range(8):
        row_values = []
        for second in range(8):
            if second == first:
                row_values.append(0.0)
            else:
                row_values.append(
                    barycentric[second]
                    / barycentric[first]
                    / (GLL_NODES[first] - GLL_NODES[second])
                )
        row_values[first] = -sum(row_values)
        matrix_rows.append(row_values)
    diff_matrix = np.array(matrix_rows)
    identity = np.eye(8)
    return np.concatenate(
        [
            np.kron(np.kron(diff_matrix, identity), identity),
            np.kron(np.kron(identity, diff_matrix), identity),
            np.kron(np.kron(identity, identity), diff_matrix),
        ],
        axis=0,
    )


def stitch_stream(gradient, from_prev, from_next):
    low_face = gradient[:, 0]
    high_face = gradient[:, 7]
    from_below = jnp.concatenate([from_prev[:, :, None, :], high_face[:, :, :-1, :]], axis=2)
    from_above = jnp.concatenate([low_face[:, :, 1:, :], from_next[:, :, None, :]], axis=2)
    return gradient.at[:, 0].set(low_face + from_below).at[:, 7].set(high_face + from_above)


def stitch_cross(gradient):
    cross_count = gradient.shape[-1]
    column = jnp.arange(cross_count, dtype=jnp.int32)
    normal = column // EZN
    spanwise = column % EZN
    low_face = gradient[:, :, 0]
    high_face = gradient[:, :, 7]
    from_below = jnp.where(normal > 0, jnp.roll(high_face, EZN, axis=-1), 0.0)
    from_above = jnp.where(normal < EYN - 1, jnp.roll(low_face, -EZN, axis=-1), 0.0)
    gradient = (
        gradient.at[:, :, 0].set(low_face + from_below).at[:, :, 7].set(high_face + from_above)
    )
    low_face = gradient[:, :, :, 0]
    high_face = gradient[:, :, :, 7]
    from_before = jnp.where(
        spanwise == 0, jnp.roll(high_face, 1 - EZN, axis=-1), jnp.roll(high_face, 1, axis=-1)
    )
    from_after = jnp.where(
        spanwise == EZN - 1, jnp.roll(low_face, EZN - 1, axis=-1), jnp.roll(low_face, -1, axis=-1)
    )
    gradient = (
        gradient.at[:, :, :, 0]
        .set(low_face + from_before)
        .at[:, :, :, 7]
        .set(high_face + from_after)
    )
    points = jnp.arange(8, dtype=jnp.int32)
    on_face = (points == 0) | (points == 7)
    at_wall = (points[:, None] == 0) & (normal[None, :] == 0) | (points[:, None] == 7) & (
        normal[None, :] == EYN - 1
    )
    edge_factor = jnp.where(on_face, 0.5, 1.0).astype(jnp.float32)
    normal_factor = jnp.where(on_face[:, None] & jnp.logical_not(at_wall), 0.5, 1.0).astype(
        jnp.float32
    )
    factors = (
        edge_factor[:, None, None, None, None]
        * normal_factor[None, :, None, None, :]
        * edge_factor[None, None, :, None, None]
    )
    return gradient * factors[None]


def middle_eigen(gradient):
    strain = [
        [0.5 * (gradient[first][second] + gradient[second][first]) for second in range(3)]
        for first in range(3)
    ]
    rotation = [
        [0.5 * (gradient[first][second] - gradient[second][first]) for second in range(3)]
        for first in range(3)
    ]
    moment = [
        [
            sum(
                (
                    strain[first][inner] * strain[inner][second]
                    + rotation[first][inner] * rotation[inner][second]
                    for inner in range(3)
                )
            )
            for second in range(3)
        ]
        for first in range(3)
    ]
    mean_diag = (moment[0][0] + moment[1][1] + moment[2][2]) / 3.0
    shift_x = moment[0][0] - mean_diag
    shift_y = moment[1][1] - mean_diag
    shift_z = moment[2][2] - mean_diag
    offdiag = (
        moment[0][1] * moment[0][1] + moment[0][2] * moment[0][2] + moment[1][2] * moment[1][2]
    )
    spread = (shift_x * shift_x + shift_y * shift_y + shift_z * shift_z + 2.0 * offdiag) / 6.0
    determinant = (
        shift_x * (shift_y * shift_z - moment[1][2] * moment[1][2])
        - moment[0][1] * (moment[0][1] * shift_z - moment[1][2] * moment[0][2])
        + moment[0][2] * (moment[0][1] * moment[1][2] - shift_y * moment[0][2])
    )
    halfdet = 0.5 * determinant
    discrim = jnp.maximum(spread * spread * spread - halfdet * halfdet, 0.0)
    angles = jnp.arctan2(jnp.sqrt(discrim), halfdet) / 3.0
    radius = 2.0 * jnp.sqrt(spread)
    largest = mean_diag + radius * jnp.cos(angles)
    smallest = mean_diag + radius * jnp.cos(angles + 2.0 * math.pi / 3.0)
    return 3.0 * mean_diag - largest - smallest


def resample(lambda_two, weight_x, weight_y, weight_z):
    highest = lax.Precision.HIGHEST
    along_x = jnp.einsum("oaie,ijke->oajke", weight_x, lambda_two, precision=highest)
    along_y = jnp.einsum("obje,oajke->oabke", weight_y, along_x, precision=highest)
    along_z = jnp.einsum("ocke,oabke->oabce", weight_z, along_y, precision=highest)
    columns = lambda_two.shape[-1]
    return jnp.transpose(along_z.reshape(2, 128, columns), (0, 2, 1))


def pack_rows(values, owners, blocks, devices, slot_count):
    onehot = (owners[:, None] == jnp.arange(devices, dtype=jnp.int32)[None, :]).astype(jnp.int32)
    ordinal = jnp.sum((jnp.cumsum(onehot, axis=0) - 1) * onehot, axis=1)
    sendbuf = jnp.zeros((devices, slot_count, 128), jnp.float32).at[owners, ordinal].set(values)
    indices = jnp.zeros((devices, slot_count), jnp.int32).at[owners, ordinal].set(blocks)
    return (sendbuf, indices)


def shards(
    velocity,
    inverse_sizes,
    resample_x,
    resample_y,
    resample_z,
    piece_target,
    target_brick,
    target_block,
    brick_home,
):
    elements = velocity.shape[2]
    cross_count = EYN * EZN
    layers = elements // cross_count
    operator = jnp.asarray(derivative_operator(), jnp.float32).astype(jnp.bfloat16)
    products = jnp.einsum("pq,cqe->cpe", operator, velocity, preferred_element_type=jnp.float32)
    gradient = (products.reshape(3, 3, 512, elements) * inverse_sizes[None, :, None, :]).reshape(
        9, 8, 64, layers, cross_count
    )
    rim_faces = jnp.stack([gradient[:, 0, :, 0, :], gradient[:, 7, :, layers - 1, :]], axis=2)
    padded = extended(rim_faces, (("dom", 2),), 1)
    from_prev = padded[:, :, 0, :]
    from_next = padded[:, :, 3, :]
    gradient = stitch_stream(gradient, from_prev, from_next)
    gradient = stitch_cross(gradient.reshape(9, 8, 8, 8, layers, cross_count))
    lambda_two = middle_eigen(gradient.reshape(3, 3, 512, elements))
    pieces = resample(
        lambda_two.reshape(8, 8, 8, elements), resample_x, resample_y, resample_z
    ).reshape(-1, 128)
    devices = lax.axis_size("dom")
    capacity = max(2, 4 * elements // devices)
    local_ids = piece_target.reshape(-1)
    owners = brick_home[target_brick[local_ids, 0]]
    sendbuf, indices = pack_rows(pieces, owners, target_block[local_ids], devices, 2 * capacity)
    received, received_blocks = (
        lax.all_to_all(sendbuf, "dom", split_axis=0, concat_axis=0, tiled=True),
        lax.all_to_all(indices, "dom", split_axis=0, concat_axis=0, tiled=True),
    )
    brick_image = (
        jnp.zeros((BLOCKS, 128), jnp.float32)
        .at[received_blocks.reshape(-1)]
        .add(received.reshape(-1, 128))
    )
    return brick_image[None]


def solution(mesh):
    return jax.shard_map(
        shards,
        mesh=mesh,
        in_specs=(
            P(None, None, "dom"),
            P(None, "dom"),
            P(None, None, None, "dom"),
            P(None, None, None, "dom"),
            P(None, None, None, "dom"),
            P(None, "dom"),
            P("dom", None),
            P("dom"),
            P(),
        ),
        out_specs=P("dom", None, None),
        check_vma=False,
    )
```

profile of v0, /device:TPU:0, one launch (start us, length us, event | category | flops | bytes accessed | tf_op | source)
XLA Modules:
  0.0 757.9 jit_solution(2298811111013023950)
XLA Ops:
  1.4 6.5 convolution_bitcast_fusion.2
  7.9 11.9 %reshape.765 = f32[9,8,64,4,128]{4,3,2,1,0:T(4,128)} reshape(f32[3,1536,512]{2,1,0:T(8,128)} %convolution_bitcast_fusion.2) | data formatting | bytes 18874368 | tf_op jit(solution)/shard_map/reshape | solution.py:204
  19.9 5.1 copy_multiply_fusion
  26.3 5.9 collective-permute-start.1
  33.7 6.5 gather_fusion
  40.2 4.5 compare_select_fusion.5
  45.0 15.7 %select_select_fusion = s32[1024]{0:T(1024)S(1)} fusion(pred[1024]{0:T(1024)(128)(4,1)S(1)} %get-tuple-element.101, pred[1024]{0:T(1024)(128)(4,1)S(1)} %get-tuple-element.100, pred[1024]{0:T(1024)(128)(4,1)S(1)} %get-tuple-element.99, pred[1024]{0:T(1024)(128)(4,1)S(1)} %get-tuple-element.98, pred[1024]{0:T(1024)(128)(4,1)S(1)} %get-tuple-element.97, ...), kind=kLoop, calls=%fused_computation.154 | loop fusion | flops 25600 | bytes 33892 | tf_op jit(solution)/shard_map/gather | solution.py:220
  60.7 9.0 %reduce-window.6 = s32[32,8,128]{2,1,0:T(8,128)S(1)} reduce-window(s32[32,8,128]{2,1,0:T(8,128)S(1)} %fusion.38, s32[]{:T(128)} %constant.226.clone.1), window={size=1x1x128 pad=0_0x0_0x127_0}, to_apply=%region_0.0 | reduce-window | flops 4161536 | bytes 262148 | tf_op jit(solution)/shard_map/reduce-window
  70.5 6.9 gather_fusion.1
  77.4 4.9 scatter_custom_fusion.1
  82.2 3.8 all-to-all-start
  89.4 4.5 copy.111
  100.0 4.7 copy.82
  105.2 3.3 copy-done.6
  108.9 3.7 copy.145
  122.3 2.9 copy.93
  127.2 6.7 fusion.5
  144.5 4.1 fusion.13
  148.5 30.6 %scatter.49 = f32[9,8,8,8,4,128]{5,3,2,4,1,0:T(8,128)} dynamic-update-slice(f32[9,8,8,8,4,128]{5,3,2,4,1,0:T(8,128)} %copy-done.5, f32[9,8,8,1,4,128]{5,3,2,4,1,0:T(1,128)} %bitcast.272, s32[]{:T(128)} %constant.226.clone.1, s32[]{:T(128)} %constant.226.clone.1, s32[]{:T(128)} %constant.226.clone.1, s32[]{:T(128)} %constant.226.clone.1, s32[]{:T(128)} %constant.226.clone.1, s32[]{:T(128)} %constant.226.clone.1) | dynamic-update-slice | bytes 2359300 | tf_op jit(solution)/shard_map/scatter | solution.py:106
  179.1 30.6 %scatter.50 = f32[9,8,8,8,4,128]{5,3,2,4,1,0:T(8,128)} dynamic-update-slice(f32[9,8,8,8,4,128]{5,3,2,4,1,0:T(8,128)} %scatter.49, f32[9,8,8,1,4,128]{5,3,2,4,1,0:T(1,128)S(1)} %get-tuple-element.117, s32[]{:T(128)} %constant.226.clone.1, s32[]{:T(128)} %constant.226.clone.1, s32[]{:T(128)} %constant.226.clone.1, s32[]{:T(128)} %constant.232.clone.1, s32[]{:T(128)} %constant.226.clone.1, ...) | dynamic-update-slice | bytes 2359300 | tf_op jit(solution)/shard_map/scatter | solution.py:108
  209.7 4.9 broadcast_multiply_fusion
  220.2 10.3 %subtract_bitcast_fusion = f32[8,8,8,512,1]{3,2,1,0,4:T(8,128)S(1)} fusion(f32[1,8,8,8,4,128]{5,3,2,4,1,0:T(8,128)S(1)} %get-tuple-element.114, f32[1,8,8,8,4,128]{5,3,2,4,1,0:T(8,128)S(1)} %get-tuple-element.116, f32[1,8,8,8,4,128]{5,3,2,4,1,0:T(8,128)S(1)} %get-tuple-element.113, f32[1,8,8,8,4,128]{5,3,2,4,1,0:T(8,128)S(1)} %get-tuple-element.115, ...), kind=kLoop, calls=%fused_computation.79 | loop fusion | flops 12320768 | bytes 7340032 | tf_op jit(solution)/shard_map/sub | solution.py:168
  230.5 13.5 %copy.110 = f32[8,8,8,512,1]{0,2,4,1,3:T(8,128)} copy(f32[8,8,8,512,1]{3,2,1,0,4:T(8,128)S(1)} %subtract_bitcast_fusion) | data formatting | bytes 2097152 | tf_op jit(solution)/shard_map/sub | solution.py:168
  244.0 80.9 %convolution_bitcast_fusion = f32[2,8,8,8,512]{1,3,0,2,4:T(8,128)} fusion(f32[8,8,8,512,1]{0,2,4,1,3:T(8,128)} %copy.110, f32[2,8,8,512,1]{2,1,0,4,3:T(8,128)} %copy.111), kind=kOutput, calls=%fused_computation.7 | convolution fusion | flops 50331648 | bytes 3407872 | tf_op jit(solution)/shard_map/oaie,ijke->oajke/dot_general | solution.py:173
  324.9 33.1 %copy.104 = f32[2,8,8,8,512]{3,2,1,4,0:T(8,128)} copy(f32[2,8,8,8,512]{1,3,0,2,4:T(8,128)} %convolution_bitcast_fusion) | data formatting | bytes 4194304 | tf_op jit(solution)/shard_map/oaie,ijke->oajke/transpose | solution.py:173
  358.0 34.0 %convolution_bitcast_fusion.1 = f32[2,8,4,8,512]{3,2,1,4,0:T(4,128)} fusion(f32[2,8,8,8,512]{3,2,1,4,0:T(8,128)} %copy.104, f32[2,4,8,512,1]{2,1,4,3,0:T(4,128)} %copy.112), kind=kOutput, calls=%fused_computation.8 | convolution fusion | flops 25165824 | bytes 3276800 | tf_op jit(solution)/shard_map/obje,oajke->oabke/dot_general | solution.py:174
  392.0 272.1 %fusion.2 = f32[2,8,4,4,512]{1,3,2,4,0:T(4,128)} fusion(f32[2,4,8,512,1]{2,1,4,3,0:T(4,128)S(1)} %copy-done.7, f32[2,8,4,8,512]{3,2,1,4,0:T(4,128)} %convolution_bitcast_fusion.1), kind=kOutput, calls=%fused_computation.12 | convolution fusion | flops 12582912 | bytes 1703936 | tf_op jit(solution)/shard_map/ocke,oabke->oabce/dot_general | solution.py:175
  664.2 6.9 copy.108
  671.3 4.5 scatter_custom_fusion.2
  675.8 6.1 all-to-all-start.1
  681.9 48.8 %all-to-all-done.1 = f32[32,128,128]{2,1,0:T(8,128)} async-done(((f32[32,128,128]{2,1,0:T(8,128)}), f32[32,128,128]{2,1,0:T(8,128)}, u32[]{:S(2)}, u32[]{:S(2)}) %all-to-all-start.1) | async-done | bytes 2097184 | tf_op jit(solution)/shard_map/all_to_all | solution.py:223
  730.8 26.8 %scatter_custom_fusion = f32[2048,128]{1,0:T(8,128)} fusion(s32[4096]{0:T(1024)S(1)} %bitcast.289, f32[4096,128]{1,0:T(8,128)} %bitcast.94, f32[]{:T(128)} %constant.225.clone.1), kind=kCustom, calls=%fused_computation.100 | custom fusion | flops 524288 | bytes 1049088 | tf_op jit(solution)/shard_map/scatter-add | solution.py:229
  (100 shorter events, 43.5 us)
Async XLA Ops:
  0.0 1.4 copy-start
  7.9 11.9 %copy-start.13 = (f32[3,512]{1,0:T(4,128)S(1)}, f32[3,512]{1,0:T(4,128)}, u32[]{:S(2)}) copy-start(f32[3,512]{1,0:T(4,128)} %param.23) | copy-start | bytes 18436
  24.9 8.7 %copy-start.4 = (f32[9,8,64,4,128]{4,2,0,3,1:T(8,128)}, f32[9,8,64,4,128]{4,2,0,3,1:T(8,128)S(1)}, u32[]{:S(2)}) copy-start(f32[9,8,64,4,128]{4,2,0,3,1:T(8,128)S(1)} %copy_multiply_fusion) | copy-start | bytes 28311556
  24.9 7.2 copy-start.10
  25.0 8.7 %copy-start.14 = (s32[2,512]{1,0:T(2,128)S(1)}, s32[2,512]{1,0:T(2,128)}, u32[]{:S(2)}) copy-start(s32[2,512]{1,0:T(2,128)} %param.27) | copy-start | bytes 12292
  25.0 8.7 %copy-start.2 = (s32[512,1]{0,1:T(1,128)S(1)}, s32[512,1]{0,1:T(1,128)}, u32[]{:S(2)}) copy-start(s32[512,1]{0,1:T(1,128)} %param.28) | copy-start | bytes 6148
  25.8 71.5 %collective-permute-start = (f32[9,64,1,128]{3,1,0,2:T(8,128)}, f32[9,64,1,128]{3,1,0,2:T(8,128)S(1)}, u32[]{:S(2)}, u32[]{:S(2)}) collective-permute-start(f32[9,64,1,128]{3,1,0,2:T(8,128)} %get-tuple-element.125), channel_id=1, source_target_pairs={{0,1},{1,2},{2,3},{3,4},{4,5},{5,6},{6,7},{7,8},{8,9},{9,10},{10,1... | collective-permute-start | bytes 884744 | tf_op jit(solution)/shard_map/ppermute | solution.py:33
  26.3 78.4 %collective-permute-start.1 = (f32[9,64,1,128]{3,1,0,2:T(8,128)}, f32[9,64,1,128]{3,1,0,2:T(8,128)S(1)}, u32[]{:S(2)}, u32[]{:S(2)}) collective-permute-start(f32[9,64,1,128]{3,1,0,2:T(8,128)} %get-tuple-element.124), channel_id=1, source_target_pairs={{1,0},{2,1},{3,2},{4,3},{5,4},{6,5},{7,6},{8,7},{9,8},{10,9},{11,1... | collective-permute-start | bytes 884744 | tf_op jit(solution)/shard_map/ppermute | solution.py:35
  40.2 30.1 %copy-start.16 = (s32[2]{0:T(128)S(1)}, s32[2]{0:T(128)}, u32[]{:S(2)}) copy-start(s32[2]{0:T(128)} %constant.246) | copy-start | bytes 28
  40.2 30.2 %copy-start.15 = (s32[2]{0:T(128)S(1)}, s32[2]{0:T(128)}, u32[]{:S(2)}) copy-start(s32[2]{0:T(128)} %constant.249) | copy-start | bytes 28
  40.2 30.3 %copy-start.3 = (s32[512]{0:T(512)S(1)}, s32[512]{0:T(512)}, u32[]{:S(2)}) copy-start(s32[512]{0:T(512)} %param.29) | copy-start | bytes 6148
  82.2 593.6 %all-to-all-start = ((s32[32,1,128]{2,1,0:T(1,128)}), s32[32,1,128]{2,1,0:T(1,128)S(1)}, u32[]{:S(2)}, u32[]{:S(2)}) async-start(s32[32,1,128]{2,1,0:T(1,128)} %bitcast.41), calls=%async_computation | async-start | bytes 32768 | tf_op jit(solution)/shard_map/all_to_all | solution.py:224
  89.4 4.5 copy-start.11
  93.8 1.7 copy-start.12
  104.9 3.6 copy-start.6
  115.3 4.0 copy-start.5
  125.2 1.8 copy-start.8
  125.2 2.0 copy-start.9
  358.0 34.0 %copy-start.7 = (f32[2,4,8,512,1]{2,1,4,3,0:T(4,128)S(1)}, f32[2,4,8,512,1]{2,1,4,3,0:T(4,128)}, u32[]{:S(2)}) copy-start(f32[2,4,8,512,1]{2,1,4,3,0:T(4,128)} %copy.113) | copy-start | bytes 393220
  675.8 55.0 %all-to-all-start.1 = ((f32[32,128,128]{2,1,0:T(8,128)}), f32[32,128,128]{2,1,0:T(8,128)}, u32[]{:S(2)}, u32[]{:S(2)}) async-start(f32[32,128,128]{2,1,0:T(8,128)} %bitcast.270), calls=%async_computation.1 | async-start | bytes 4194304 | tf_op jit(solution)/shard_map/all_to_all | solution.py:223
  681.9 75.7 %copy-start.1 = (bf16[3,512,512]{2,1,0:T(8,128)(2,1)S(1)}, bf16[3,512,512]{2,1,0:T(8,128)(2,1)}, u32[]{:S(2)}) copy-start(bf16[3,512,512]{2,1,0:T(8,128)(2,1)} %param.22) | copy-start | bytes 4718596
where the time goes:
time: 767 us; the launch traced here: 758 us
  matrix products  394 us (51%)
  local copies, waits for them, and re-layouts  198 us (26%)
  other arithmetic  101 us (13%)
  waiting for transfers between devices  48.8 us (6%)
  starting transfers between devices  16.3 us (2%)
    dot_general x1, matrix products, resample(): jnp.einsum('ocke,oabke->oabce', weight_z, along_y, precision=highest)  272 us
    dot_general x1, matrix products, resample(): jnp.einsum('oaie,ijke->oajke', weight_x, lambda_two, precision=highest)  80.9 us
    scatter x2, local copies, waits for them, and re-layouts, stitch_cross(): gradient = gradient.at[:, :, :, 0].set(low_face + from_before).at[:, :, :...  61.2 us
    all_to_all x1, waiting for transfers between devices, shards(): lax.all_to_all(sendbuf, 'dom', split_axis=0, concat_axis=0, tiled=True)  48.8 us
    dot_general x1, matrix products, resample(): jnp.einsum('obje,oajke->oabke', weight_y, along_x, precision=highest)  34 us
    transpose x1, local copies, waits for them, and re-layouts, resample(): jnp.einsum('oaie,ijke->oajke', weight_x, lambda_two, precision=highest)  33.1 us
    scatter-add x1, other arithmetic, shards(): brick_image = jnp.zeros((BLOCKS, 128), jnp.float32).at[received_blocks.re...  26.8 us
    unnamed x41, local copies, waits for them, and re-layouts  26.6 us
  transfers between devices with their start and end apart: 4, of which 1 were waited for; matrix products, arithmetic and copies ran while one was open for 84% of the time, Pallas kernels for 0%

commit v1 on v0

v1 whole, which is shorter than its diff:
```python
import functools
import math

import jax
import jax.numpy as jnp
import ml_dtypes
import numpy as np
from jax import lax
from jax.experimental import pallas as pl
from jax.experimental.pallas import tpu as pltpu
from jax.sharding import PartitionSpec as P

EYN = 8
EZN = 16
CROSS = EYN * EZN
BLOCKS = 2048
F32 = jnp.float32
BF16 = jnp.bfloat16

GLL_NODES = [
    -1.0,
    -0.8717401485096066,
    -0.5917001814331423,
    -0.2092992179024789,
    0.2092992179024789,
    0.5917001814331423,
    0.8717401485096066,
    1.0,
]

ORDER = [0, 1, 2, 3, 7, 4, 5, 6]


def derivative_operator():
    barycentric = []
    for first in range(8):
        product_term = 1.0
        for other in range(8):
            if other != first:
                product_term = product_term * (GLL_NODES[first] - GLL_NODES[other])
        barycentric.append(1.0 / product_term)
    matrix_rows = []
    for first in range(8):
        row_values = []
        for second in range(8):
            if second == first:
                row_values.append(0.0)
            else:
                row_values.append(
                    barycentric[second]
                    / barycentric[first]
                    / (GLL_NODES[first] - GLL_NODES[second])
                )
        row_values[first] = -sum(row_values)
        matrix_rows.append(row_values)
    diff_matrix = np.array(matrix_rows)
    identity = np.eye(8)
    return np.concatenate(
        [
            np.kron(np.kron(diff_matrix, identity), identity),
            np.kron(np.kron(identity, diff_matrix), identity),
            np.kron(np.kron(identity, identity), diff_matrix),
        ],
        axis=0,
    )


def operators():
    rounded = derivative_operator().astype(np.float32).astype(ml_dtypes.bfloat16).astype(np.float32)
    ends = np.ones(8, np.float32)
    ends[0] = ends[7] = 0.5
    halves = ends[:, None, None] * ends[None, :, None] * ends[None, None, :]
    rows = rounded.reshape(3, 8, 8, 8, 512) * halves[None, :, :, :, None]
    rows = rows.transpose(0, 2, 3, 1, 4)[:, :, ORDER]
    whole = rows[:, :, :, ORDER].reshape(3, 512, 512)
    faces = np.stack([rows[:, :, :, 0], rows[:, :, :, 7]]).reshape(384, 512)
    return whole.astype(ml_dtypes.bfloat16), faces.astype(ml_dtypes.bfloat16)


def third_angle():
    spots = (1.0 - np.cos(np.pi * (np.arange(4000) + 0.5) / 4000)) / 2
    values = np.sin(np.arcsin(1.0 - spots * spots) / 3.0)
    fitted = np.polynomial.chebyshev.Chebyshev.fit(spots, values, 9, domain=[0, 1])
    return [float(c) for c in fitted.convert(kind=np.polynomial.Polynomial).coef]


THIRD = third_angle()


def dot(left, right):
    return lax.dot_general(left, right, (((1,), (0,)), ((), ())), preferred_element_type=F32)


def dot_nt(left, right):
    return lax.dot_general(left, right, (((1,), (1,)), ((), ())), preferred_element_type=F32)


def iota(shape, axis):
    return lax.broadcasted_iota(jnp.int32, shape, axis)


def onehot(mask):
    return jnp.where(mask, 1.0, 0.0).astype(BF16)


def halves_of(values):
    high = values.astype(BF16)
    return high, (values - high.astype(F32)).astype(BF16)


def normal_sums(low, high):
    normal = iota(low.shape, 1) // EZN
    below = pltpu.roll(high, EZN, 1)
    above = pltpu.roll(low, CROSS - EZN, 1)
    return (
        low + jnp.where(normal == 0, low, below),
        high + jnp.where(normal == EYN - 1, high, above),
    )


def from_before(values):
    spanwise = iota(values.shape, 1) % EZN
    return jnp.where(
        spanwise == 0, pltpu.roll(values, CROSS + 1 - EZN, 1), pltpu.roll(values, 1, 1)
    )


def from_after(values):
    spanwise = iota(values.shape, 1) % EZN
    return jnp.where(
        spanwise == EZN - 1, pltpu.roll(values, EZN - 1, 1), pltpu.roll(values, CROSS - 1, 1)
    )


def rim_kernel(faces_ref, first_ref, last_ref, sizes_first, sizes_last, lo_first, hi_first, lo_last, hi_last):
    sub = iota((64, CROSS), 0) % 8
    for vel, sizes, outs in (
        (first_ref, sizes_first, (lo_first, hi_first)),
        (last_ref, sizes_last, (lo_last, hi_last)),
    ):
        for c in range(3):
            products = dot(faces_ref[...], vel[c])
            for face in range(2):
                for a in range(3):
                    at = (face * 3 + a) * 64
                    part = products[at : at + 64] * sizes[a : a + 1, :]
                    low, high = normal_sums(part[:8], part[56:])
                    part = jnp.concatenate([low, part[8:56], high], axis=0)
                    swapped = jnp.where(sub == 0, from_after(part), from_before(part))
                    swapped = pltpu.roll(swapped.reshape(8, 8, CROSS), 4, 1).reshape(64, CROSS)
                    part = part + jnp.where((sub == 0) | (sub == 4), swapped, 0.0)
                    outs[face][pl.ds((c * 3 + a) * 64, 64), :] = part


def route_kernel(capacity, pt_ref, brick_ref, block_ref, home_ref, slot_ref, ids_ref):
    targets = brick_ref.shape[1]
    bricks = home_ref.shape[0]
    devices = ids_ref.shape[0]
    named = iota((bricks, targets), 0) == brick_ref[...]
    named_f = jnp.where(named, 1.0, 0.0)
    earlier = onehot(iota((targets, targets), 0) < iota((targets, targets), 1))
    ranks = dot(named_f.astype(BF16), earlier)
    owner = jnp.sum(named_f * home_ref[...].astype(F32), axis=0, keepdims=True)
    rank = jnp.sum(named_f * ranks, axis=0, keepdims=True)
    row = iota((8, targets), 0)
    both = jnp.where(row == 0, owner, jnp.where(row == 1, rank, 0.0)).astype(BF16)
    for o in range(2):
        picked = onehot(iota((targets, targets), 0) == pt_ref[o : o + 1, :])
        found = dot(both, picked)
        slot_ref[o : o + 1, :] = (found[0:1] * capacity + found[1:2]).astype(jnp.int32)
    owned = jnp.where(iota((devices, targets), 0) == owner.astype(jnp.int32), 1.0, 0.0)
    placed = onehot(iota((capacity, targets), 0) == rank.astype(jnp.int32))
    block = block_ref[...]
    upper = (block // 64).astype(F32)
    lower = (block % 64).astype(F32)
    ids = (
        dot_nt((owned * upper).astype(BF16), placed) * 64.0
        + dot_nt((owned * lower).astype(BF16), placed)
        + dot_nt(owned.astype(BF16), placed)
        - 1.0
    )
    ids_ref[...] = ids.astype(jnp.int32)


def middle_eigen(g):
    s01, s02, s12 = g[0][1] + g[1][0], g[0][2] + g[2][0], g[1][2] + g[2][1]
    p01, p02, p12 = g[0][1] * g[1][0], g[0][2] * g[2][0], g[1][2] * g[2][1]
    m00 = g[0][0] * g[0][0] + (p01 + p02)
    m11 = g[1][1] * g[1][1] + (p01 + p12)
    m22 = g[2][2] * g[2][2] + (p02 + p12)
    m01 = 0.5 * ((g[0][0] + g[1][1]) * s01 + g[0][2] * g[2][1] + g[1][2] * g[2][0])
    m02 = 0.5 * ((g[0][0] + g[2][2]) * s02 + g[0][1] * g[1][2] + g[2][1] * g[1][0])
    m12 = 0.5 * ((g[1][1] + g[2][2]) * s12 + g[1][0] * g[0][2] + g[2][0] * g[0][1])
    q = (m00 + m11 + m22) * (1.0 / 3.0)
    x, y, z = m00 - q, m11 - q, m22 - q
    n01, n02, n12 = m01 * m01, m02 * m02, m12 * m12
    spread = (x * x + y * y + z * z + 2.0 * (n01 + n02 + n12)) * (1.0 / 6.0)
    halfdet = 0.5 * (x * (y * z - n12) - z * n01 - y * n02) + m01 * m02 * m12
    inverse = lax.rsqrt(jnp.maximum(spread, 1e-37))
    ratio = jnp.abs(halfdet) * inverse * inverse * inverse
    gap = jnp.maximum(1.0 - ratio, 1e-30)
    root = gap * lax.rsqrt(gap)
    third = THIRD[-1]
    for coefficient in THIRD[-2::-1]:
        third = third * root + coefficient
    turn = 2.0 * (spread * inverse) * third
    return jnp.where(halfdet < 0.0, q + turn, q - turn)


def slab_pieces(count, op_ref, vels, sizes, rxs, rys, rzs, belows, aboves, part, lam, along, store):
    joined = [
        jnp.concatenate([vels[l][c] for l in range(count)], axis=1) if count > 1 else vels[0][c]
        for c in range(3)
    ]
    for c in range(3):
        for a in range(3):
            products = dot(op_ref[a], joined[c])
            for l in range(count):
                part[l, pl.ds((c * 3 + a) * 512, 512), :] = (
                    products[:, l * CROSS : (l + 1) * CROSS] * sizes[l][a : a + 1, :]
                )

    def stitch(ca, l):
        at = ca * 512
        low, high = normal_sums(part[l, pl.ds(at, 64), :], part[l, pl.ds(at + 448, 64), :])
        part[l, pl.ds(at, 64), :] = low
        part[l, pl.ds(at + 448, 64), :] = high
        for j in range(8):
            near, far = pl.ds(at + j * 64, 8), pl.ds(at + j * 64 + 32, 8)
            low, high = part[l, near, :], part[l, far, :]
            part[l, near, :] = low + from_before(high)
            part[l, far, :] = high + from_after(low)

    for l in range(count):
        lax.fori_loop(0, 9, lambda ca, carry, l=l: (stitch(ca, l), carry)[1], 0)

    def face_row(source, which, l, ca, jk):
        if source is not None:
            return source[pl.ds(ca * 64 + jk, 1), :]
        return part[l, pl.ds(ca * 512 + jk * 8 + which, 1), :]

    sub = iota((8, CROSS), 0)

    def point_row(jk, l):
        g = []
        for ca in range(9):
            below = face_row(belows[l], 4, l - 1, ca, jk)
            above = face_row(aboves[l], 0, l + 1, ca, jk)
            g.append(
                part[l, pl.ds(ca * 512 + jk * 8, 8), :]
                + jnp.where(sub == 0, below, jnp.where(sub == 4, above, 0.0))
            )
        lam[pl.ds(jk * 8, 8), :] = middle_eigen([g[0:3], g[3:6], g[6:9]])

    for l in range(count):
        lax.fori_loop(0, 64, lambda jk, carry, l=l: (point_row(jk, l), carry)[1], 0, unroll=2)
        for o in range(2):
            for j in range(8):
                rows = [lam[pl.ds((j * 8 + k) * 8, 8), :] for k in range(8)]
                for w in range(4):
                    total = rows[0] * rzs[l][o, w, ORDER[0] : ORDER[0] + 1, :]
                    for k in range(1, 8):
                        total = total + rows[k] * rzs[l][o, w, ORDER[k] : ORDER[k] + 1, :]
                    along[0, pl.ds((w * 8 + j) * 8, 8), :] = total
            for w in range(4):
                rows = [along[0, pl.ds((w * 8 + j) * 8, 8), :] for j in range(8)]
                for v in range(4):
                    total = rows[0] * rys[l][o, v, 0:1, :]
                    for j in range(1, 8):
                        total = total + rows[j] * rys[l][o, v, j : j + 1, :]
                    along[1, pl.ds((v * 4 + w) * 8, 8), :] = total
            rows = [along[1, pl.ds(i, 16, stride=8), :] for i in range(8)]
            for u in range(8):
                total = rows[0] * rxs[l][o, u, ORDER[0] : ORDER[0] + 1, :]
                for i in range(1, 8):
                    total = total + rows[i] * rxs[l][o, u, ORDER[i] : ORDER[i] + 1, :]
                high, low = halves_of(total)
                columns = pl.ds((l * 2 + o) * CROSS, CROSS)
                store[pl.ds(u * 16, 16), columns] = high
                store[pl.ds(128 + u * 16, 16), columns] = low


def split_refs(refs, count):
    groups = []
    for _ in range(5):
        groups.append(refs[:count])
        refs = refs[count:]
    return groups, refs


def inner_kernel(count, *refs):
    op_ref, refs = refs[0], refs[1:]
    (vels, sizes, rxs, rys, rzs), refs = split_refs(refs, count)
    below, above, store, lo_out, hi_out, part, lam, along = refs
    belows = [below] + [None] * (count - 1)
    aboves = [None] * (count - 1) + [above]
    slab_pieces(count, op_ref, vels, sizes, rxs, rys, rzs, belows, aboves, part, lam, along, store)
    lo_out[...] = part[0, pl.ds(0, 576, stride=8), :]
    hi_out[...] = part[count - 1, pl.ds(4, 576, stride=8), :]


def outer_kernel(layers, *refs):
    op_ref, refs = refs[0], refs[1:]
    (vels, sizes, rxs, rys, rzs), refs = split_refs(refs, 2)
    below_first, above_first, below_last, above_last, slots, inner, send, part, lam, along, store = refs
    slab_pieces(
        2, op_ref, vels, sizes, rxs, rys, rzs, [below_first, below_last], [above_first, above_last], part, lam, along, store
    )
    rows = iota((send.shape[0], CROSS), 0)

    def chosen(which):
        return jnp.concatenate(
            [
                onehot(rows == slots[o : o + 1, l * CROSS : (l + 1) * CROSS])
                for l in which
                for o in range(2)
            ],
            axis=1,
        )

    both = dot_nt(chosen(range(1, layers - 1)), inner[...]) + dot_nt(chosen((0, layers - 1)), store[...])
    send[...] = both[:, :128] + both[:, 128:]


def gather_kernel(ids_ref, rows_ref, out_ref, halves):
    high, low = halves_of(rows_ref[...])
    halves[:, :128] = high
    halves[:, 128:] = low
    step = 256

    def chunk(i, carry):
        named = onehot(iota((step, ids_ref.shape[1]), 0) + i * step == ids_ref[...])
        both = dot(named, halves[...])
        out_ref[pl.ds(pl.multiple_of(i * step, step), step), :] = both[:, :128] + both[:, 128:]
        return carry

    lax.fori_loop(0, BLOCKS // step, chunk, 0)


def params():
    return pltpu.CompilerParams(vmem_limit_bytes=48 * 1024 * 1024)


def whole_spec(shape):
    return pl.BlockSpec(shape, lambda i: (0,) * len(shape))


def layer_spec(array, layer):
    lead = array.shape[:-1]
    return pl.BlockSpec(lead + (CROSS,), lambda i: (0,) * len(lead) + (layer,))


def shards(
    velocity,
    inverse_sizes,
    resample_x,
    resample_y,
    resample_z,
    piece_target,
    target_brick,
    target_block,
    brick_home,
):
    elements = velocity.shape[2]
    layers = elements // CROSS
    devices = lax.axis_size("dom")
    capacity = max(2, 4 * elements // devices)
    whole, faces = (jnp.asarray(o) for o in operators())
    face_shape = jax.ShapeDtypeStruct((576, CROSS), F32)
    last = layers - 1

    lo_first, hi_first, lo_last, hi_last = pl.pallas_call(
        rim_kernel,
        grid=(1,),
        in_specs=[
            whole_spec(faces.shape),
            layer_spec(velocity, 0),
            layer_spec(velocity, last),
            layer_spec(inverse_sizes, 0),
            layer_spec(inverse_sizes, last),
        ],
        out_specs=[whole_spec((576, CROSS))] * 4,
        out_shape=[face_shape] * 4,
        compiler_params=params(),
        name="rim_faces",
    )(faces, velocity, velocity, inverse_sizes, inverse_sizes)
    from_prev = lax.ppermute(hi_last, "dom", [(i, (i + 1) % devices) for i in range(devices)])
    from_next = lax.ppermute(lo_first, "dom", [((i + 1) % devices, i) for i in range(devices)])

    slots, ids = pl.pallas_call(
        functools.partial(route_kernel, capacity),
        out_shape=[
            jax.ShapeDtypeStruct((2, elements), jnp.int32),
            jax.ShapeDtypeStruct((devices, capacity), jnp.int32),
        ],
        compiler_params=params(),
        name="routes",
    )(
        piece_target,
        target_brick.reshape(1, elements),
        target_block.reshape(1, elements),
        brick_home.reshape(-1, 1),
    )
    received_ids = lax.all_to_all(ids, "dom", split_axis=0, concat_axis=0, tiled=True)

    arrays = (velocity, inverse_sizes, resample_x, resample_y, resample_z)

    def scratch(count):
        return [
            pltpu.VMEM((count, 4608, CROSS), F32),
            pltpu.VMEM((512, CROSS), F32),
            pltpu.VMEM((2, 256, CROSS), F32),
        ]

    def layer_operands(which):
        specs = [layer_spec(array, l) for array in arrays for l in which]
        return specs, [array for array in arrays for _ in which]

    inside = range(1, last)
    specs, operands = layer_operands(inside)
    inner, lo_inner, hi_inner = pl.pallas_call(
        functools.partial(inner_kernel, len(inside)),
        grid=(1,),
        in_specs=[whole_spec(whole.shape)] + specs + [whole_spec((576, CROSS))] * 2,
        out_specs=[whole_spec((256, len(inside) * 256)), whole_spec((576, CROSS)), whole_spec((576, CROSS))],
        out_shape=[jax.ShapeDtypeStruct((256, len(inside) * 256), BF16), face_shape, face_shape],
        scratch_shapes=scratch(len(inside)),
        compiler_params=params(),
        name="inner_layers",
    )(whole, *operands, hi_first, lo_last)

    specs, operands = layer_operands((0, last))
    rows = devices * capacity
    sendbuf = pl.pallas_call(
        functools.partial(outer_kernel, layers),
        grid=(1,),
        in_specs=[whole_spec(whole.shape)]
        + specs
        + [whole_spec((576, CROSS))] * 4
        + [whole_spec(slots.shape), whole_spec(inner.shape)],
        out_specs=whole_spec((rows, 128)),
        out_shape=jax.ShapeDtypeStruct((rows, 128), F32),
        scratch_shapes=scratch(2) + [pltpu.VMEM((256, 512), BF16)],
        compiler_params=params(),
        name="outer_layers",
    )(whole, *operands, from_prev, lo_inner, hi_inner, from_next, slots, inner)

    received = lax.all_to_all(
        sendbuf.reshape(devices, capacity, 128), "dom", split_axis=0, concat_axis=0, tiled=True
    )
    image = pl.pallas_call(
        gather_kernel,
        out_shape=jax.ShapeDtypeStruct((BLOCKS, 128), F32),
        scratch_shapes=[pltpu.VMEM((rows, 256), BF16)],
        compiler_params=params(),
        name="block_sums",
    )(received_ids.reshape(1, rows), received.reshape(rows, 128))
    return image[None]


def solution(mesh):
    return jax.shard_map(
        shards,
        mesh=mesh,
        in_specs=(
            P(None, None, "dom"),
            P(None, "dom"),
            P(None, None, None, "dom"),
            P(None, None, None, "dom"),
            P(None, None, None, "dom"),
            P(None, "dom"),
            P("dom", None),
            P("dom"),
            P(),
        ),
        out_specs=P("dom", None, None),
        check_vma=False,
    )
```

time: 767 us -> 85.4 us (0.11); the launches traced: 758 us -> 84.8 us
  matrix products: 394 us -> 0 us
  local copies, waits for them, and re-layouts: 198 us -> 12.4 us
  other arithmetic: 101 us -> 1.43 us
  Pallas kernels: 0 us -> 31.4 us
  waiting for transfers between devices: 48.8 us -> 24.2 us
    dot_general x4 -> x0, matrix products: 394 us -> none  [the longest x1 272 us: resample(): jnp.einsum('ocke,oabke->oabce', weight_z, along_y, precision=highest)]
    scatter x3 -> x0, local copies, waits for them, and re-layouts: 65.8 us -> none  [the longest x2 61.2 us: stitch_cross(): gradient = gradient.at[:, :, :, 0].set(low_face + from_before).at[:, :, :...]
    transpose x2 -> x0, local copies, waits for them, and re-layouts: 39.9 us -> none  [the longest x1 33.1 us: resample(): jnp.einsum('oaie,ijke->oajke', weight_x, lambda_two, precision=highest)]
    pallas_call x0 -> x5, Pallas kernels: none -> 31.4 us  [the longest x1 12.6 us: shards(): pl.pallas_call(functools.partial(outer_kernel, layers), grid=(1,), in_spe...]
    scatter-add x1 -> x0, other arithmetic: 26.8 us -> none  [shards(): brick_image = jnp.zeros((BLOCKS, 128), jnp.float32).at[received_blocks.re...]
    all_to_all x2, waiting for transfers between devices: 48.8 us -> 24.1 us  [the longest x1 24.1 us: shards(): lax.all_to_all(sendbuf.reshape(devices, capacity, 128), 'dom', split_axis...]
    gather x4 -> x0, other arithmetic: 20.5 us -> none  [the longest x3 20.5 us: shards(): owners = brick_home[target_brick[local_ids, 0]]]
    add x6 -> x0, other arithmetic: 16.3 us -> none  [the longest x1 6.71 us: stitch_cross(): high_face + from_after]
  transfers between devices with their start and end apart: 4 -> 4, of which waited for: 1 -> 1; matrix products, arithmetic and copies ran while one was open for 84% -> 3% of each run, Pallas kernels for 0% -> 27%
where the time goes in v1:
time: 85.4 us; the launch traced here: 84.8 us
  Pallas kernels  31.4 us (37%)
  waiting for transfers between devices  24.2 us (28%)
  starting transfers between devices  15.3 us (18%)
  local copies, waits for them, and re-layouts  12.4 us (15%)
  other arithmetic  1.43 us (2%)
    all_to_all x1, waiting for transfers between devices, shards(): lax.all_to_all(sendbuf.reshape(devices, capacity, 128), 'dom', split_axis...  24.1 us
    pallas_call x1, Pallas kernels, shards(): pl.pallas_call(functools.partial(outer_kernel, layers), grid=(1,), in_spe...  12.6 us
    unnamed x42, local copies, waits for them, and re-layouts  11 us
    pallas_call x1, Pallas kernels, shards(): pl.pallas_call(functools.partial(inner_kernel, len(inside)), grid=(1,), i...  9.92 us
    ppermute x1, starting transfers between devices, shards(): lax.ppermute(lo_first, 'dom', [((i + 1) % devices, i) for i in range(devi...  5.92 us
    all_to_all x1, starting transfers between devices, shards(): lax.all_to_all(sendbuf.reshape(devices, capacity, 128), 'dom', split_axis...  5.77 us
    pallas_call x1, Pallas kernels, shards(): pl.pallas_call(gather_kernel, out_shape=jax.ShapeDtypeStruct((BLOCKS, 128...  4.68 us
    pallas_call x1, Pallas kernels, shards(): pl.pallas_call(rim_kernel, grid=(1,), in_specs=[whole_spec(faces.shape),...  3.7 us
  transfers between devices with their start and end apart: 4, of which 1 were waited for; matrix products, arithmetic and copies ran while one was open for 3% of the time, Pallas kernels for 27%

profile of v1, /device:TPU:0, one launch (start us, length us, event | category | flops | bytes accessed | tf_op | source)
XLA Modules:
  0.0 84.8 jit_solution(1985589079795572086)
XLA Ops:
  0.0 1.4 %copy-done = bf16[3,512,512]{2,1,0:T(8,128)(2,1)S(1)} copy-done((bf16[3,512,512]{2,1,0:T(8,128)(2,1)S(1)}, bf16[3,512,512]{2,1,0:T(8,128)(2,1)}, u32[]{:S(2)}) %copy-start) | copy-done | bytes 1572888
  1.4 1.0 %copy-done.8 = bf16[384,512]{1,0:T(8,128)(2,1)S(1)} copy-done((bf16[384,512]{1,0:T(8,128)(2,1)S(1)}, bf16[384,512]{1,0:T(8,128)(2,1)}, u32[]{:S(2)}) %copy-start.8) | copy-done | bytes 393240
  2.4 0.7 copy-done.9
  3.1 3.7 %rim_faces.1 = (f32[576,128]{1,0:T(8,128)}, f32[576,128]{1,0:T(8,128)S(1)}, f32[576,128]{1,0:T(8,128)S(1)}, f32[576,128]{1,0:T(8,128)}) custom-call(bf16[384,512]{1,0:T(8,128)(2,1)S(1)} %copy-done.8, bf16[3,512,512]{2,1,0:T(8,128)(2,1)S(1)} %copy-done, bf16[3,512,512]{2,1,0:T(8,128)(2,1)S(1)} %copy-done, f32[3,512]{1,0:T(4,128)S(1)} %copy-done.9, ...), custom_call_target="tpu_custom_call" | custom-call | tf_op jit(solution)/shard_map/rim_faces/pallas_call | solution.py:372
  6.8 0.7 copy-done.11
  7.6 0.7 copy-done.13
  8.3 0.5 collective-permute-start
  8.7 5.9 %collective-permute-start.1 = (f32[576,128]{1,0:T(8,128)}, f32[576,128]{1,0:T(8,128)}, u32[]{:S(2)}, u32[]{:S(2)}) collective-permute-start(f32[576,128]{1,0:T(8,128)} %get-tuple-element.20), channel_id=1, source_target_pairs={{1,0},{2,1},{3,2},{4,3},{5,4},{6,5},{7,6},{8,7},{9,8},{10,9},{11,1... | collective-permute-start | bytes 884744 | tf_op jit(solution)/shard_map/ppermute | solution.py:388
  14.7 0.7 copy.13.home_ref
  15.4 0.7 copy-done.15
  16.1 0.7 copy-done.18
  16.8 0.7 copy-done.19
  17.4 0.5 routes.1
  17.9 0.0 copy-start.16
  17.9 0.6 copy-done.16
  18.5 3.2 %all-to-all-start = ((s32[32,1,64]{2,1,0:T(1,128)}), s32[32,1,64]{2,1,0:T(1,128)}, u32[]{:S(2)}, u32[]{:S(2)}) async-start(s32[32,1,64]{2,1,0:T(1,128)} %bitcast.11), calls=%async_computation | async-start | bytes 32768 | tf_op jit(solution)/shard_map/all_to_all | solution.py:404
  21.8 0.0 copy-start.6
  21.8 0.9 %copy-done.6 = f32[2,4,8,512]{3,2,1,0:T(8,128)S(1)} copy-done((f32[2,4,8,512]{3,2,1,0:T(8,128)S(1)}, f32[2,4,8,512]{3,2,1,0:T(8,128)}, u32[]{:S(2)}) %copy-start.6) | copy-done | bytes 131096
  22.7 1.0 %copy-done.12 = f32[576,128]{1,0:T(8,128)S(1)} copy-done((f32[576,128]{1,0:T(8,128)S(1)}, f32[576,128]{1,0:T(8,128)}, u32[]{:S(2)}) %copy-start.12) | copy-done | bytes 294936
  23.7 1.0 %copy-done.14 = f32[576,128]{1,0:T(8,128)S(1)} copy-done((f32[576,128]{1,0:T(8,128)S(1)}, f32[576,128]{1,0:T(8,128)}, u32[]{:S(2)}) %copy-start.14) | copy-done | bytes 294936
  24.6 9.9 %inner_layers.1 = (bf16[256,512]{1,0:T(8,128)(2,1)S(1)}, f32[576,128]{1,0:T(8,128)S(1)}, f32[576,128]{1,0:T(8,128)S(1)}) custom-call(bf16[3,512,512]{2,1,0:T(8,128)(2,1)S(1)} %copy-done.2, bf16[3,512,512]{2,1,0:T(8,128)(2,1)S(1)} %copy-done.1, bf16[3,512,512]{2,1,0:T(8,128)(2,1)S(1)} %copy-done.1, f32[3,512]{1,0:T(4,128)S(1)} %copy-done.10, ...), custom_call_target="tpu_custom_call" | custom-call | tf_op jit(solution)/shard_map/inner_layers/pallas_call | solution.py:421
  34.6 0.0 collective-permute-done.refs_11_
  34.6 0.0 collective-permute-done.1.refs_14_
  34.6 12.6 %outer_layers.1 = f32[2048,128]{1,0:T(8,128)S(1)} custom-call(bf16[3,512,512]{2,1,0:T(8,128)(2,1)S(1)} %copy-done.2, bf16[3,512,512]{2,1,0:T(8,128)(2,1)S(1)} %copy-done.1, bf16[3,512,512]{2,1,0:T(8,128)(2,1)S(1)} %copy-done.1, f32[3,512]{1,0:T(4,128)S(1)} %copy-done.10, f32[3,512]{1,0:T(4,128)S(1)} %copy-done.10, f32[2,8,8,512]{3,2,1,0:T(8,128)S(1)} %copy-done.3, ...), custom_call_target="tpu_custom_call" | custom-call | tf_op jit(solution)/shard_map/outer_layers/pallas_call | solution.py:434
  47.2 0.0 copy-start.4
  47.2 1.0 %copy-done.4 = f32[2048,128]{1,0:T(8,128)} copy-done((f32[2048,128]{1,0:T(8,128)}, f32[2048,128]{1,0:T(8,128)S(1)}, u32[]{:S(2)}) %copy-start.4) | copy-done | bytes 1048600
  48.1 5.8 %all-to-all-start.1 = ((f32[32,64,128]{2,1,0:T(8,128)}), f32[32,64,128]{2,1,0:T(8,128)S(1)}, u32[]{:S(2)}, u32[]{:S(2)}) async-start(f32[32,64,128]{2,1,0:T(8,128)} %bitcast.9), calls=%async_computation.1 | async-start | bytes 2097152 | tf_op jit(solution)/shard_map/all_to_all | solution.py:448
  53.9 0.6 broadcast.3
  54.5 1.4 %reduce.3 = s32[32,64]{1,0:T(8,128)S(1)} reduce(s32[32,1,64]{2,1,0:T(1,128)} %all-to-all-done, s32[]{:T(128)} %broadcast.3), dimensions={1}, to_apply=%all_to_all.10.reduce_sub_computation.3 | reduce | bytes 16388 | tf_op jit(solution)/shard_map/all_to_all | solution.py:404
  55.9 0.1 reshape.24.ids_ref
  56.0 24.1 %all-to-all-done.1 = f32[32,64,128]{2,1,0:T(8,128)S(1)} async-done(((f32[32,64,128]{2,1,0:T(8,128)}), f32[32,64,128]{2,1,0:T(8,128)S(1)}, u32[]{:S(2)}, u32[]{:S(2)}) %all-to-all-start.1) | async-done | bytes 1048608 | tf_op jit(solution)/shard_map/all_to_all | solution.py:448
  80.2 4.7 %block_sums.1 = f32[2048,128]{1,0:T(8,128)} custom-call(s32[1,2048]{1,0:T(1,128)S(1)} %reshape.24.ids_ref, f32[2048,128]{1,0:T(8,128)S(1)} %bitcast.10), custom_call_target="tpu_custom_call" | custom-call | tf_op jit(solution)/shard_map/block_sums/pallas_call | solution.py:451
  (27 shorter events, 0.0 us)
Async XLA Ops:
  0.0 1.4 %copy-start = (bf16[3,512,512]{2,1,0:T(8,128)(2,1)S(1)}, bf16[3,512,512]{2,1,0:T(8,128)(2,1)}, u32[]{:S(2)}) copy-start(bf16[3,512,512]{2,1,0:T(8,128)(2,1)} %refs_2_.3) | copy-start | bytes 4718596
  1.4 1.0 %copy-start.8 = (bf16[384,512]{1,0:T(8,128)(2,1)S(1)}, bf16[384,512]{1,0:T(8,128)(2,1)}, u32[]{:S(2)}) copy-start(bf16[384,512]{1,0:T(8,128)(2,1)} %constant.5.clone.faces_ref) | copy-start | bytes 1179652
  2.4 0.7 copy-start.9
  3.1 11.6 %copy-start.20 = (s32[32]{0:T(128)S(1)}, s32[32]{0:T(128)}, u32[]{:S(2)}) copy-start(s32[32]{0:T(128)} %param.19) | copy-start | bytes 388
  3.1 12.2 %copy-start.17 = (s32[2,512]{1,0:T(2,128)S(1)}, s32[2,512]{1,0:T(2,128)}, u32[]{:S(2)}) copy-start(s32[2,512]{1,0:T(2,128)} %pt_ref.1) | copy-start | bytes 12292
  3.1 18.6 %copy-start.1 = (bf16[3,512,512]{2,1,0:T(8,128)(2,1)S(1)}, bf16[3,512,512]{2,1,0:T(8,128)(2,1)}, u32[]{:S(2)}) copy-start(bf16[3,512,512]{2,1,0:T(8,128)(2,1)} %refs_2_.3) | copy-start | bytes 4718596
  3.1 18.6 %copy-start.2 = (bf16[3,512,512]{2,1,0:T(8,128)(2,1)S(1)}, bf16[3,512,512]{2,1,0:T(8,128)(2,1)}, u32[]{:S(2)}) copy-start(bf16[3,512,512]{2,1,0:T(8,128)(2,1)} %constant.4.clone.refs_0_) | copy-start | bytes 4718596
  3.1 18.6 %copy-start.3 = (f32[2,8,8,512]{3,2,1,0:T(8,128)S(1)}, f32[2,8,8,512]{3,2,1,0:T(8,128)}, u32[]{:S(2)}) copy-start(f32[2,8,8,512]{3,2,1,0:T(8,128)} %refs_6_.3) | copy-start | bytes 786436
  3.1 18.6 %copy-start.5 = (f32[2,4,8,512]{3,2,1,0:T(8,128)S(1)}, f32[2,4,8,512]{3,2,1,0:T(8,128)}, u32[]{:S(2)}) copy-start(f32[2,4,8,512]{3,2,1,0:T(8,128)} %refs_8_.3) | copy-start | bytes 393220
  3.1 18.6 %copy-start.10 = (f32[3,512]{1,0:T(4,128)S(1)}, f32[3,512]{1,0:T(4,128)}, u32[]{:S(2)}) copy-start(f32[3,512]{1,0:T(4,128)} %refs_4_.3) | copy-start | bytes 18436
  6.8 0.7 copy-start.11
  7.6 0.7 copy-start.13
  8.3 26.3 %collective-permute-start = (f32[576,128]{1,0:T(8,128)}, f32[576,128]{1,0:T(8,128)}, u32[]{:S(2)}, u32[]{:S(2)}) collective-permute-start(f32[576,128]{1,0:T(8,128)} %get-tuple-element.15), channel_id=1, source_target_pairs={{0,1},{1,2},{2,3},{3,4},{4,5},{5,6},{6,7},{7,8},{8,9},{9,10},{10,1... | collective-permute-start | bytes 884744 | tf_op jit(solution)/shard_map/ppermute | solution.py:387
  8.7 25.8 %collective-permute-start.1 = (f32[576,128]{1,0:T(8,128)}, f32[576,128]{1,0:T(8,128)}, u32[]{:S(2)}, u32[]{:S(2)}) collective-permute-start(f32[576,128]{1,0:T(8,128)} %get-tuple-element.20), channel_id=1, source_target_pairs={{1,0},{2,1},{3,2},{4,3},{5,4},{6,5},{7,6},{8,7},{9,8},{10,9},{11,1... | collective-permute-start | bytes 884744 | tf_op jit(solution)/shard_map/ppermute | solution.py:388
  15.4 0.7 copy-start.15
  16.1 0.7 copy-start.18
  16.8 0.7 copy-start.19
  17.9 0.6 copy-start.16
  18.5 29.6 %all-to-all-start = ((s32[32,1,64]{2,1,0:T(1,128)}), s32[32,1,64]{2,1,0:T(1,128)}, u32[]{:S(2)}, u32[]{:S(2)}) async-start(s32[32,1,64]{2,1,0:T(1,128)} %bitcast.11), calls=%async_computation | async-start | bytes 32768 | tf_op jit(solution)/shard_map/all_to_all | solution.py:404
  21.8 0.9 %copy-start.6 = (f32[2,4,8,512]{3,2,1,0:T(8,128)S(1)}, f32[2,4,8,512]{3,2,1,0:T(8,128)}, u32[]{:S(2)}) copy-start(f32[2,4,8,512]{3,2,1,0:T(8,128)} %refs_10_.3) | copy-start | bytes 393220
  22.7 1.0 %copy-start.12 = (f32[576,128]{1,0:T(8,128)S(1)}, f32[576,128]{1,0:T(8,128)}, u32[]{:S(2)}) copy-start(f32[576,128]{1,0:T(8,128)} %copy-done.11) | copy-start | bytes 884740
  23.7 1.0 %copy-start.14 = (f32[576,128]{1,0:T(8,128)S(1)}, f32[576,128]{1,0:T(8,128)}, u32[]{:S(2)}) copy-start(f32[576,128]{1,0:T(8,128)} %copy-done.13) | copy-start | bytes 884740
  24.6 10.0 %copy-start.7 = (f32[2,4,8,512]{3,2,1,0:T(8,128)S(1)}, f32[2,4,8,512]{3,2,1,0:T(8,128)}, u32[]{:S(2)}) copy-start(f32[2,4,8,512]{3,2,1,0:T(8,128)} %refs_10_.3) | copy-start | bytes 393220
  47.2 1.0 %copy-start.4 = (f32[2048,128]{1,0:T(8,128)}, f32[2048,128]{1,0:T(8,128)S(1)}, u32[]{:S(2)}) copy-start(f32[2048,128]{1,0:T(8,128)S(1)} %outer_layers.1) | copy-start | bytes 3145732
  48.1 32.0 %all-to-all-start.1 = ((f32[32,64,128]{2,1,0:T(8,128)}), f32[32,64,128]{2,1,0:T(8,128)S(1)}, u32[]{:S(2)}, u32[]{:S(2)}) async-start(f32[32,64,128]{2,1,0:T(8,128)} %bitcast.9), calls=%async_computation.1 | async-start | bytes 2097152 | tf_op jit(solution)/shard_map/all_to_all | solution.py:448

commit v2 on v1

v2 whole, which is shorter than its diff:
```python
import functools
import math

import jax
import jax.numpy as jnp
import ml_dtypes
import numpy as np
from jax import lax
from jax.experimental import pallas as pl
from jax.experimental.pallas import tpu as pltpu
from jax.sharding import PartitionSpec as P

EYN = 8
EZN = 16
CROSS = EYN * EZN
BLOCKS = 2048
F32 = jnp.float32
BF16 = jnp.bfloat16

GLL_NODES = [
    -1.0,
    -0.8717401485096066,
    -0.5917001814331423,
    -0.2092992179024789,
    0.2092992179024789,
    0.5917001814331423,
    0.8717401485096066,
    1.0,
]

ORDER = [0, 1, 2, 3, 7, 4, 5, 6]


def derivative_operator():
    barycentric = []
    for first in range(8):
        product_term = 1.0
        for other in range(8):
            if other != first:
                product_term = product_term * (GLL_NODES[first] - GLL_NODES[other])
        barycentric.append(1.0 / product_term)
    matrix_rows = []
    for first in range(8):
        row_values = []
        for second in range(8):
            if second == first:
                row_values.append(0.0)
            else:
                row_values.append(
                    barycentric[second]
                    / barycentric[first]
                    / (GLL_NODES[first] - GLL_NODES[second])
                )
        row_values[first] = -sum(row_values)
        matrix_rows.append(row_values)
    diff_matrix = np.array(matrix_rows)
    identity = np.eye(8)
    return np.concatenate(
        [
            np.kron(np.kron(diff_matrix, identity), identity),
            np.kron(np.kron(identity, diff_matrix), identity),
            np.kron(np.kron(identity, identity), diff_matrix),
        ],
        axis=0,
    )


def operators():
    rounded = derivative_operator().astype(np.float32).astype(ml_dtypes.bfloat16).astype(np.float32)
    ends = np.ones(8, np.float32)
    ends[0] = ends[7] = 0.5
    halves = ends[:, None, None] * ends[None, :, None] * ends[None, None, :]
    rows = rounded.reshape(3, 8, 8, 8, 512) * halves[None, :, :, :, None]
    rows = rows.transpose(0, 2, 3, 1, 4)[:, :, ORDER]
    whole = rows[:, :, :, ORDER].reshape(3, 512, 512)
    faces = np.stack([rows[:, :, :, 0], rows[:, :, :, 7]]).reshape(384, 512)
    return whole.astype(ml_dtypes.bfloat16), faces.astype(ml_dtypes.bfloat16)


def third_angle():
    spots = (1.0 - np.cos(np.pi * (np.arange(4000) + 0.5) / 4000)) / 2
    values = np.sin(np.arcsin(1.0 - spots * spots) / 3.0)
    fitted = np.polynomial.chebyshev.Chebyshev.fit(spots, values, 9, domain=[0, 1])
    return [float(c) for c in fitted.convert(kind=np.polynomial.Polynomial).coef]


THIRD = third_angle()


def dot(left, right):
    return lax.dot_general(left, right, (((1,), (0,)), ((), ())), preferred_element_type=F32)


def dot_nt(left, right):
    return lax.dot_general(left, right, (((1,), (1,)), ((), ())), preferred_element_type=F32)


def iota(shape, axis):
    return lax.broadcasted_iota(jnp.int32, shape, axis)


def onehot(mask):
    return jnp.where(mask, 1.0, 0.0).astype(BF16)


def halves_of(values):
    high = values.astype(BF16)
    return high, (values - high.astype(F32)).astype(BF16)


def normal_sums(low, high):
    normal = iota(low.shape, 1) // EZN
    below = pltpu.roll(high, EZN, 1)
    above = pltpu.roll(low, CROSS - EZN, 1)
    return (
        low + jnp.where(normal == 0, low, below),
        high + jnp.where(normal == EYN - 1, high, above),
    )


def span_lanes(step):
    lane = iota((8, CROSS), 1)
    return lane // EZN * EZN + (lane + step) % EZN


def moved(values, lanes):
    index = jnp.broadcast_to(lanes[None], (values.shape[0] // 8, 8, CROSS)).reshape(values.shape)
    return jnp.take_along_axis(values, index, axis=1, mode="promise_in_bounds")


def rim_kernel(last, faces_hbm, vel_hbm, sizes_hbm, lo_first, hi_first, lo_last, hi_last, faces, vel, sizes, made, sems):
    tiles = ((last, (lo_last, hi_last)), (0, (lo_first, hi_first)))
    copies = []

    def begin(source, target):
        copy = pltpu.make_async_copy(source, target, sems.at[len(copies)])
        copy.start()
        copies.append(copy)
        return copy

    waits = [begin(faces_hbm, faces)]
    for n, (l, _) in enumerate(tiles):
        columns = pl.ds(l * CROSS, CROSS)
        waits.append(begin(vel_hbm.at[:, :, columns], vel.at[n]))
        waits.append(begin(sizes_hbm.at[:, columns], sizes.at[n]))
    sub = iota((64, CROSS), 0) % 8
    before, after = span_lanes(EZN - 1), span_lanes(1)
    waits[0].wait()
    results = []
    for n, (l, outs) in enumerate(tiles):
        waits[1 + 2 * n].wait()
        waits[2 + 2 * n].wait()
        for c in range(3):
            products = dot(faces[...], vel[n, c])
            for face in range(2):
                for a in range(3):
                    at = (face * 3 + a) * 64
                    part = products[at : at + 64] * sizes[n, a : a + 1, :]
                    low, high = normal_sums(part[:8], part[56:])
                    part = jnp.concatenate([low, part[8:56], high], axis=0)
                    swapped = jnp.where(sub == 0, moved(part, after), moved(part, before))
                    swapped = pltpu.roll(swapped.reshape(8, 8, CROSS), 4, 1).reshape(64, CROSS)
                    part = part + jnp.where((sub == 0) | (sub == 4), swapped, 0.0)
                    made[n, face, pl.ds((c * 3 + a) * 64, 64), :] = part
        for face in range(2):
            results.append(begin(made.at[n, face], outs[face]))
    for copy in results:
        copy.wait()


def routes(devices, capacity, pt_ref, brick_ref, block_ref, home_ref):
    targets = brick_ref.shape[1]
    bricks = home_ref.shape[1]
    named = jnp.where(iota((bricks, targets), 0) == brick_ref[...], 1.0, 0.0)
    earlier = onehot(iota((targets, targets), 0) < iota((targets, targets), 1))
    ranks = dot(named.astype(BF16), earlier)
    homes = jnp.broadcast_to(home_ref[...].astype(F32), (8, bricks)).astype(BF16)
    owner = dot(homes, named.astype(BF16))[0:1]
    rank = jnp.sum(named * ranks, axis=0, keepdims=True)
    row = iota((8, targets), 0)
    both = jnp.where(row == 0, owner, jnp.where(row == 1, rank, 0.0)).astype(BF16)
    slots = []
    for o in range(2):
        picked = onehot(iota((targets, targets), 0) == pt_ref[o : o + 1, :])
        found = dot(both, picked)
        slots.append((found[0:1] * (capacity + 1) + found[1:2]).astype(jnp.int32))
    owned = jnp.where(iota((devices, targets), 0) == owner.astype(jnp.int32), 1.0, 0.0)
    placed = onehot(iota((128, targets), 0) == rank.astype(jnp.int32))
    block = block_ref[...]
    upper = (block // 64).astype(F32)
    lower = (block % 64).astype(F32)
    ids = (
        dot_nt((owned * upper).astype(BF16), placed) * 64.0
        + dot_nt((owned * lower).astype(BF16), placed)
        + dot_nt(owned.astype(BF16), placed)
        - 1.0
    )
    return slots, ids


def middle_eigen(g):
    s01, s02, s12 = g[0][1] + g[1][0], g[0][2] + g[2][0], g[1][2] + g[2][1]
    p01, p02, p12 = g[0][1] * g[1][0], g[0][2] * g[2][0], g[1][2] * g[2][1]
    m00 = g[0][0] * g[0][0] + (p01 + p02)
    m11 = g[1][1] * g[1][1] + (p01 + p12)
    m22 = g[2][2] * g[2][2] + (p02 + p12)
    m01 = 0.5 * ((g[0][0] + g[1][1]) * s01 + (g[0][2] * g[2][1] + g[1][2] * g[2][0]))
    m02 = 0.5 * ((g[0][0] + g[2][2]) * s02 + (g[0][1] * g[1][2] + g[2][1] * g[1][0]))
    m12 = 0.5 * ((g[1][1] + g[2][2]) * s12 + (g[1][0] * g[0][2] + g[2][0] * g[0][1]))
    q = (m00 + m11 + m22) * (1.0 / 3.0)
    x, y, z = m00 - q, m11 - q, m22 - q
    n01, n02, n12 = m01 * m01, m02 * m02, m12 * m12
    spread = (x * x + y * y + z * z + 2.0 * (n01 + n02 + n12)) * (1.0 / 6.0)
    halfdet = 0.5 * (x * (y * z - n12) - z * n01 - y * n02) + m01 * m02 * m12
    inverse = lax.rsqrt(jnp.maximum(spread, 1e-37))
    ratio = ((jnp.abs(halfdet) * inverse) * inverse) * inverse
    gap = jnp.maximum(1.0 - ratio, 1e-30)
    root = gap * lax.rsqrt(gap)
    pairs = [THIRD[n] + THIRD[n + 1] * root for n in range(0, 10, 2)]
    square = root * root
    fourth = square * square
    third = (pairs[0] + pairs[1] * square) + fourth * (
        (pairs[2] + pairs[3] * square) + fourth * pairs[4]
    )
    turn = 2.0 * (spread * inverse) * third
    return jnp.where(halfdet < 0.0, q + turn, q - turn)


def layer_pieces(layers, arrays, waits, belows, aboves, part, lam, along, store, before_stitch):
    op, vel, sizes, rx, ry, rz = arrays
    count = len(layers)
    lanes = [slice(l * CROSS, (l + 1) * CROSS) for l in layers]

    def joined(read):
        if layers[-1] - layers[0] == count - 1:
            return read(slice(lanes[0].start, lanes[-1].stop))
        return jnp.concatenate([read(at) for at in lanes], axis=1)

    before, after = span_lanes(EZN - 1), span_lanes(1)
    for c in range(3):
        velocities = joined(lambda at: vel[c, :, at])
        for a in range(3):
            products = dot(op[a], velocities) * joined(lambda at: sizes[a : a + 1, at])
            for l in range(count):
                values = products[:, l * CROSS : (l + 1) * CROSS]
                first, final = normal_sums(values[:64], values[448:])
                for j in range(8):
                    rows = {0: first, 7: final}.get(j, values[j * 64 : (j + 1) * 64])
                    near, far = rows[:8], rows[32:40]
                    at = (c * 3 + a) * 512 + j * 64
                    part[l, pl.ds(at, 8), :] = near + moved(far, before)
                    part[l, pl.ds(at + 8, 24), :] = rows[8:32]
                    part[l, pl.ds(at + 32, 8), :] = far + moved(near, after)
                    part[l, pl.ds(at + 40, 24), :] = rows[40:]
    before_stitch()
    for copy in waits:
        copy.wait()

    def face_sums(ca, carry):
        near, far = pl.ds(ca * 512, 64, stride=8), pl.ds(ca * 512 + 4, 64, stride=8)
        rows = pl.ds(ca * 64, 64)
        for l in range(count):
            if belows[l] is not None:
                part[l, near, :] = part[l, near, :] + belows[l][rows, :]
            if aboves[l] is not None:
                part[l, far, :] = part[l, far, :] + aboves[l][rows, :]
            else:
                shared = part[l, far, :] + part[l + 1, near, :]
                part[l, far, :] = shared
                part[l + 1, near, :] = shared
        return carry

    lax.fori_loop(0, 9, face_sums, 0, unroll=3)

    def point_row(jk, l):
        g = [part[l, pl.ds(ca * 512 + jk * 8, 8), :] for ca in range(9)]
        lam[pl.ds(jk * 8, 8), :] = middle_eigen([g[0:3], g[3:6], g[6:9]])

    for l in range(count):
        lax.fori_loop(0, 64, lambda jk, carry, l=l: (point_row(jk, l), carry)[1], 0, unroll=16)
        cols = lanes[l]
        for o in range(2):
            for j in range(8):
                rows = [lam[pl.ds((j * 8 + k) * 8, 8), :] for k in range(8)]
                for w in range(4):
                    total = rows[0] * rz[o, w, ORDER[0] : ORDER[0] + 1, cols]
                    for k in range(1, 8):
                        total = total + rows[k] * rz[o, w, ORDER[k] : ORDER[k] + 1, cols]
                    along[0, pl.ds((w * 8 + j) * 8, 8), :] = total
            for w in range(4):
                rows = [along[0, pl.ds((w * 8 + j) * 8, 8), :] for j in range(8)]
                for v in range(4):
                    total = rows[0] * ry[o, v, 0:1, cols]
                    for j in range(1, 8):
                        total = total + rows[j] * ry[o, v, j : j + 1, cols]
                    along[1, pl.ds((v * 4 + w) * 8, 8), :] = total
            rows = [along[1, pl.ds(i, 16, stride=8), :] for i in range(8)]
            for u in range(8):
                total = rows[0] * rx[o, u, ORDER[0] : ORDER[0] + 1, cols]
                for i in range(1, 8):
                    total = total + rows[i] * rx[o, u, ORDER[i] : ORDER[i] + 1, cols]
                high, low = halves_of(total)
                columns = pl.ds((l * 2 + o) * CROSS, CROSS)
                store[pl.ds(u * 16, 16), columns] = high
                store[pl.ds(128 + u * 16, 16), columns] = low


def started(pairs, sems):
    copies = [pltpu.make_async_copy(source, target, sems.at[n]) for n, (source, target) in enumerate(pairs)]
    for copy in copies:
        copy.start()
    return copies


def inner_kernel(layers, *refs):
    arrays, (below_hbm, above_hbm, store, lo_out, hi_out, below, above, part, lam, along, sems) = refs[:6], refs[6:]
    count = len(layers)
    waits = started([(below_hbm, below), (above_hbm, above)], sems)

    def give_faces():
        lo_out[...] = part[0, pl.ds(0, 576, stride=8), :]
        hi_out[...] = part[count - 1, pl.ds(4, 576, stride=8), :]

    belows = [below] + [None] * (count - 1)
    aboves = [None] * (count - 1) + [above]
    layer_pieces(layers, arrays, waits, belows, aboves, part, lam, along, store, give_faces)


def outer_kernel(last, devices, capacity, *refs):
    arrays, (above_first, below_last, inner), hbm, send_hbm = refs[:6], refs[6:9], refs[9:15], refs[15]
    local, (part, lam, along, store, send, sems) = refs[16:22], refs[22:]
    waits = started(list(zip(hbm, local)), sems)
    below_first, above_last = local[:2]
    layer_pieces(
        (0, last), arrays, waits, [below_first, below_last], [above_first, above_last], part, lam, along, store, lambda: None
    )
    slots, ids = routes(devices, capacity, *local[2:])
    numbers = jnp.concatenate(halves_of(ids), axis=1)
    total = send.shape[0]
    parts = 4 if total % 32 == 0 else 1
    size = total // parts
    outs = []
    for n in range(parts):
        rows = iota((size, CROSS), 0) + n * size

        def chosen(which):
            return jnp.concatenate(
                [onehot(rows == slots[o][:, l * CROSS : (l + 1) * CROSS]) for l in which for o in range(2)], axis=1
            )

        homes = iota((size, devices), 1) * (capacity + 1) + capacity
        numbered = onehot(iota((size, devices), 0) + n * size == homes)
        both = dot_nt(chosen(range(1, last)), inner[...]) + dot_nt(chosen((0, last)), store[...]) + dot(numbered, numbers)
        at = pl.ds(n * size, size)
        send[at, :] = both[:, :128] + both[:, 128:]
        copy = pltpu.make_async_copy(send.at[at], send_hbm.at[at], sems.at[6 + n])
        copy.start()
        outs.append(copy)
    for copy in outs:
        copy.wait()


def gather_kernel(devices, capacity, rows_ref, out_hbm, halves, ids, image, sems):
    total = devices * (capacity + 1)
    wide = halves.shape[0]
    high, low = halves_of(rows_ref[...])
    halves[:total, :128] = high
    halves[:total, 128:] = low
    if wide > total:
        halves[total:, :] = jnp.zeros((wide - total, 256), BF16)
    numbers = rows_ref[pl.ds(capacity, devices, stride=capacity + 1), :]
    column = iota((128, wide), 1)
    spread = onehot(iota((128, wide), 0) == column % (capacity + 1))
    high, low = halves_of(numbers)
    tiled = dot(high, spread) + dot(low, spread)
    at = iota((devices, wide), 1)
    mine = (at // (capacity + 1) == iota((devices, wide), 0)) & (at % (capacity + 1) < capacity)
    found = jnp.sum(jnp.where(mine, tiled + 1.0, 0.0), axis=0, keepdims=True) - 1.0
    ids[...] = found.astype(jnp.int32)
    step = 256
    outs = []
    for n in range(BLOCKS // step):
        named = onehot(iota((step, wide), 0) + n * step == ids[...])
        both = dot(named, halves[...])
        at = pl.ds(n * step, step)
        image[at, :] = both[:, :128] + both[:, 128:]
        copy = pltpu.make_async_copy(image.at[at], out_hbm.at[at], sems.at[n])
        copy.start()
        outs.append(copy)
    for copy in outs:
        copy.wait()


def params():
    return pltpu.CompilerParams(vmem_limit_bytes=24 * 1024 * 1024)


FAR = pl.BlockSpec(memory_space=pltpu.HBM)
NEAR = pl.BlockSpec(memory_space=pltpu.VMEM)


def shards(
    velocity,
    inverse_sizes,
    resample_x,
    resample_y,
    resample_z,
    piece_target,
    target_brick,
    target_block,
    brick_home,
):
    elements = velocity.shape[2]
    last = elements // CROSS - 1
    devices = lax.axis_size("dom")
    capacity = max(2, 4 * elements // devices)
    whole, faces = (jnp.asarray(o) for o in operators())
    face = (576, CROSS)
    face_shape = jax.ShapeDtypeStruct(face, F32)

    lo_first, hi_first, lo_last, hi_last = pl.pallas_call(
        functools.partial(rim_kernel, last),
        in_specs=[FAR] * 3,
        out_specs=[FAR] * 4,
        out_shape=[face_shape] * 4,
        scratch_shapes=[
            pltpu.VMEM(faces.shape, BF16),
            pltpu.VMEM((2, 3, 512, CROSS), BF16),
            pltpu.VMEM((2, 3, CROSS), F32),
            pltpu.VMEM((2, 2) + face, F32),
            pltpu.SemaphoreType.DMA((9,)),
        ],
        compiler_params=params(),
        name="rim_faces",
    )(faces, velocity, inverse_sizes)
    from_prev = lax.ppermute(hi_last, "dom", [(i, (i + 1) % devices) for i in range(devices)])
    from_next = lax.ppermute(lo_first, "dom", [((i + 1) % devices, i) for i in range(devices)])

    arrays = (whole, velocity, inverse_sizes, resample_x, resample_y, resample_z)

    def scratch(count):
        return [
            pltpu.VMEM((count, 4608, CROSS), F32),
            pltpu.VMEM((512, CROSS), F32),
            pltpu.VMEM((2, 256, CROSS), F32),
        ]

    inside = tuple(range(1, last))
    inner, lo_inner, hi_inner = pl.pallas_call(
        functools.partial(inner_kernel, inside),
        in_specs=[NEAR] * 6 + [FAR] * 2,
        out_specs=[NEAR] * 3,
        out_shape=[jax.ShapeDtypeStruct((256, len(inside) * 256), BF16), face_shape, face_shape],
        scratch_shapes=[pltpu.VMEM(face, F32)] * 2 + scratch(len(inside)) + [pltpu.SemaphoreType.DMA((2,))],
        compiler_params=params(),
        name="inner_layers",
    )(*arrays, hi_first, lo_last)

    rows = devices * (capacity + 1)
    routing = (
        piece_target,
        target_brick.reshape(1, elements),
        target_block.reshape(1, elements),
        brick_home.reshape(1, -1),
    )
    sendbuf = pl.pallas_call(
        functools.partial(outer_kernel, last, devices, capacity),
        in_specs=[NEAR] * 9 + [FAR] * 6,
        out_specs=FAR,
        out_shape=jax.ShapeDtypeStruct((rows, 128), F32),
        scratch_shapes=[pltpu.VMEM(face, F32)] * 2
        + [pltpu.VMEM(array.shape, array.dtype) for array in routing]
        + scratch(2)
        + [pltpu.VMEM((256, 512), BF16), pltpu.VMEM((rows, 128), F32), pltpu.SemaphoreType.DMA((10,))],
        compiler_params=params(),
        name="outer_layers",
    )(*arrays, lo_inner, hi_inner, inner, from_prev, from_next, *routing)

    received = lax.all_to_all(
        sendbuf.reshape(devices, 1, (capacity + 1) * 128), "dom", split_axis=0, concat_axis=0, tiled=True
    )
    wide = -(-rows // 128) * 128
    image = pl.pallas_call(
        functools.partial(gather_kernel, devices, capacity),
        in_specs=[NEAR],
        out_specs=FAR,
        out_shape=jax.ShapeDtypeStruct((BLOCKS, 128), F32),
        scratch_shapes=[
            pltpu.VMEM((wide, 256), BF16),
            pltpu.VMEM((1, wide), jnp.int32),
            pltpu.VMEM((BLOCKS, 128), F32),
            pltpu.SemaphoreType.DMA((8,)),
        ],
        compiler_params=params(),
        name="block_sums",
    )(received.reshape(rows, 128))
    return image[None]


def solution(mesh):
    return jax.shard_map(
        shards,
        mesh=mesh,
        in_specs=(
            P(None, None, "dom"),
            P(None, "dom"),
            P(None, None, None, "dom"),
            P(None, None, None, "dom"),
            P(None, None, None, "dom"),
            P(None, "dom"),
            P("dom", None),
            P("dom"),
            P(),
        ),
        out_specs=P("dom", None, None),
        check_vma=False,
    )
```

time: 85.4 us -> 63.5 us (0.74)
  blocking collectives: 0 us -> 31.1 us
  waiting for transfers between devices: 24.2 us -> 0.01 us
  Pallas kernels: 31.4 us -> 19.9 us
  starting transfers between devices: 15.3 us -> 6.49 us
  local copies, waits for them, and re-layouts: 12.4 us -> 5.43 us
  other arithmetic: 1.43 us -> 0 us
    all_to_all x0 -> x1, blocking collectives: none -> 31.1 us  [shards(): lax.all_to_all(sendbuf.reshape(devices, 1, (capacity + 1) * 128), 'dom',...]
    all_to_all x2 -> x0, waiting for transfers between devices: 24.1 us -> none  [the longest x1 24.1 us: shards(): lax.all_to_all(sendbuf.reshape(devices, capacity, 128), 'dom', split_axis...]
    pallas_call x5 -> x4, Pallas kernels: 31.4 us -> 19.9 us  [the longest x1 8.92 us: shards(): pl.pallas_call(functools.partial(outer_kernel, last, devices, capacity),...]
    all_to_all x2 -> x0, starting transfers between devices: 8.97 us -> none  [the longest x1 5.77 us: shards(): lax.all_to_all(sendbuf.reshape(devices, capacity, 128), 'dom', split_axis...]
    unnamed x42 -> x24, local copies, waits for them, and re-layouts: 11 us -> 5.43 us
    all_to_all x1 -> x0, other arithmetic: 1.43 us -> none  [shards(): lax.all_to_all(ids, 'dom', split_axis=0, concat_axis=0, tiled=True)]
  transfers between devices with their start and end apart: 4 -> 2, of which waited for: 1 -> 0; matrix products, arithmetic and copies ran while one was open for 3% -> 0% of each run, Pallas kernels for 27% -> 8%
where the time goes in v2:
time: 63.5 us; the launch traced here: 63.2 us
  blocking collectives  31.1 us (49%)
  Pallas kernels  19.9 us (31%)
  starting transfers between devices  6.49 us (10%)
  local copies, waits for them, and re-layouts  5.43 us (9%)
    all_to_all x1, blocking collectives, shards(): lax.all_to_all(sendbuf.reshape(devices, 1, (capacity + 1) * 128), 'dom',...  31.1 us
    pallas_call x1, Pallas kernels, shards(): pl.pallas_call(functools.partial(outer_kernel, last, devices, capacity),...  8.92 us
    ppermute x1, starting transfers between devices, shards(): lax.ppermute(lo_first, 'dom', [((i + 1) % devices, i) for i in range(devi...  5.99 us
    unnamed x24, local copies, waits for them, and re-layouts  5.43 us
    pallas_call x1, Pallas kernels, shards(): pl.pallas_call(functools.partial(inner_kernel, inside), in_specs=[NEAR] *...  4.75 us
    pallas_call x1, Pallas kernels, shards(): pl.pallas_call(functools.partial(gather_kernel, devices, capacity), in_sp...  3.76 us
    pallas_call x1, Pallas kernels, shards(): pl.pallas_call(functools.partial(rim_kernel, last), in_specs=[FAR] * 3, o...  2.48 us
  transfers between devices with their start and end apart: 2, of which 0 were waited for; matrix products, arithmetic and copies ran while one was open for 0% of the time, Pallas kernels for 8%

profile of v2, /device:TPU:0, one launch (start us, length us, event | category | flops | bytes accessed | tf_op | source)
XLA Modules:
  0.0 63.2 jit_solution(13037357089919614180)
XLA Ops:
  0.0 0.0 copy-start
  0.0 1.4 %copy-done = bf16[3,512,512]{2,1,0:T(8,128)(2,1)S(1)} copy-done((bf16[3,512,512]{2,1,0:T(8,128)(2,1)S(1)}, bf16[3,512,512]{2,1,0:T(8,128)(2,1)}, u32[]{:S(2)}) %copy-start) | copy-done | bytes 1572888
  1.4 0.0 copy-start.6
  1.4 1.0 %copy-done.6 = bf16[384,512]{1,0:T(8,128)(2,1)S(1)} copy-done((bf16[384,512]{1,0:T(8,128)(2,1)S(1)}, bf16[384,512]{1,0:T(8,128)(2,1)}, u32[]{:S(2)}) %copy-start.6) | copy-done | bytes 393240
  2.4 0.0 copy-start.7
  2.4 0.7 %copy-done.7 = f32[3,512]{1,0:T(4,128)S(1)} copy-done((f32[3,512]{1,0:T(4,128)S(1)}, f32[3,512]{1,0:T(4,128)}, u32[]{:S(2)}) %copy-start.7) | copy-done | bytes 6168
  3.1 0.0 copy-start.1
  3.1 0.0 copy-start.3
  3.1 0.0 copy-start.4
  3.1 2.5 %rim_faces.1 = (f32[576,128]{1,0:T(8,128)S(1)}, f32[576,128]{1,0:T(8,128)S(1)}, f32[576,128]{1,0:T(8,128)S(1)}, f32[576,128]{1,0:T(8,128)S(1)}) custom-call(bf16[384,512]{1,0:T(8,128)(2,1)S(1)} %copy-done.6, bf16[3,512,512]{2,1,0:T(8,128)(2,1)S(1)} %copy-done, f32[3,512]{1,0:T(4,128)S(1)} %copy-done.7), custom_call_target="tpu_custom_call" | custom-call | tf_op jit(solution)/shard_map/rim_faces/pallas_call | solution.py:421
  5.6 0.5 collective-permute-start
  6.1 6.0 %collective-permute-start.1 = (f32[576,128]{1,0:T(8,128)S(1)}, f32[576,128]{1,0:T(8,128)S(1)}, u32[]{:S(2)}, u32[]{:S(2)}) collective-permute-start(f32[576,128]{1,0:T(8,128)S(1)} %get-tuple-element.18), channel_id=1, source_target_pairs={{1,0},{2,1},{3,2},{4,3},{5,4},{6,5},{7,6},{8,7},{9,8},{10,9},{11,1... | collective-permute-start | bytes 884744 | tf_op jit(solution)/shard_map/ppermute | solution.py:437
  12.1 0.0 copy-done.1
  12.1 0.0 copy-done.3
  12.1 0.0 copy-done.4
  12.1 0.0 copy-start.2
  12.1 1.4 %copy-done.2 = bf16[3,512,512]{2,1,0:T(8,128)(2,1)S(1)} copy-done((bf16[3,512,512]{2,1,0:T(8,128)(2,1)S(1)}, bf16[3,512,512]{2,1,0:T(8,128)(2,1)}, u32[]{:S(2)}) %copy-start.2) | copy-done | bytes 1572888
  13.5 0.0 copy-start.5
  13.5 0.9 %copy-done.5 = f32[2,4,8,512]{3,2,1,0:T(8,128)S(1)} copy-done((f32[2,4,8,512]{3,2,1,0:T(8,128)S(1)}, f32[2,4,8,512]{3,2,1,0:T(8,128)}, u32[]{:S(2)}) %copy-start.5) | copy-done | bytes 131096
  14.4 0.0 copy-start.8
  14.4 0.0 copy-start.9
  14.4 0.0 copy-start.10
  14.4 4.8 %inner_layers.1 = (bf16[256,512]{1,0:T(8,128)(2,1)S(1)}, f32[576,128]{1,0:T(8,128)S(1)}, f32[576,128]{1,0:T(8,128)S(1)}) custom-call(bf16[3,512,512]{2,1,0:T(8,128)(2,1)S(1)} %copy-done.2, bf16[3,512,512]{2,1,0:T(8,128)(2,1)S(1)} %copy-done.1, f32[3,512]{1,0:T(4,128)S(1)} %copy-done.7, f32[2,8,8,512]{3,2,1,0:T(8,128)S(1)} %copy-done.3, ...), custom_call_target="tpu_custom_call" | custom-call | tf_op jit(solution)/shard_map/inner_layers/pallas_call | solution.py:449
  19.2 0.0 collective-permute-done.refs_9_
  19.2 0.0 collective-permute-done.1.refs_10_
  19.2 0.0 copy-done.8
  19.2 0.0 copy-done.9
  19.2 0.0 copy-done.10
  19.2 0.0 copy-done.11
  19.2 8.9 %outer_layers.1 = f32[2080,128]{1,0:T(8,128)S(1)} custom-call(bf16[3,512,512]{2,1,0:T(8,128)(2,1)S(1)} %copy-done.2, bf16[3,512,512]{2,1,0:T(8,128)(2,1)S(1)} %copy-done.1, f32[3,512]{1,0:T(4,128)S(1)} %copy-done.7, f32[2,8,8,512]{3,2,1,0:T(8,128)S(1)} %copy-done.3, f32[2,4,8,512]{3,2,1,0:T(8,128)S(1)} %copy-done.4, f32[2,4,8,512]{3,2,1,0:T(8,128)S(1)} %copy-done.5, ...), custom_call_target="tpu_custom_call" | custom-call | tf_op jit(solution)/shard_map/outer_layers/pallas_call | solution.py:466
  28.2 31.1 %all_to_all.5 = f32[32,1,8320]{2,1,0:T(1,128)S(1)} all-to-all(f32[32,1,8320]{2,1,0:T(1,128)S(1)} %bitcast.6), channel_id=1, replica_groups=mesh['dom'=32] {'dom'}, dimensions={0} | all-to-all | bytes 2129920 | tf_op jit(solution)/shard_map/all_to_all | solution.py:479
  59.3 3.8 %block_sums.1 = f32[2048,128]{1,0:T(8,128)} custom-call(f32[2080,128]{1,0:T(8,128)S(1)} %bitcast.7), custom_call_target="tpu_custom_call" | custom-call | tf_op jit(solution)/shard_map/block_sums/pallas_call | solution.py:483
  (1 shorter events, 0.0 us)
Async XLA Ops:
  0.0 1.4 %copy-start = (bf16[3,512,512]{2,1,0:T(8,128)(2,1)S(1)}, bf16[3,512,512]{2,1,0:T(8,128)(2,1)}, u32[]{:S(2)}) copy-start(bf16[3,512,512]{2,1,0:T(8,128)(2,1)} %refs_1_.3) | copy-start | bytes 4718596
  1.4 1.0 %copy-start.6 = (bf16[384,512]{1,0:T(8,128)(2,1)S(1)}, bf16[384,512]{1,0:T(8,128)(2,1)}, u32[]{:S(2)}) copy-start(bf16[384,512]{1,0:T(8,128)(2,1)} %constant.5.clone.faces_hbm) | copy-start | bytes 1179652
  2.4 0.7 %copy-start.7 = (f32[3,512]{1,0:T(4,128)S(1)}, f32[3,512]{1,0:T(4,128)}, u32[]{:S(2)}) copy-start(f32[3,512]{1,0:T(4,128)} %refs_2_.3) | copy-start | bytes 18436
  3.1 9.0 %copy-start.1 = (bf16[3,512,512]{2,1,0:T(8,128)(2,1)S(1)}, bf16[3,512,512]{2,1,0:T(8,128)(2,1)}, u32[]{:S(2)}) copy-start(bf16[3,512,512]{2,1,0:T(8,128)(2,1)} %refs_1_.3) | copy-start | bytes 4718596
  3.1 9.0 %copy-start.3 = (f32[2,8,8,512]{3,2,1,0:T(8,128)S(1)}, f32[2,8,8,512]{3,2,1,0:T(8,128)}, u32[]{:S(2)}) copy-start(f32[2,8,8,512]{3,2,1,0:T(8,128)} %refs_3_.3) | copy-start | bytes 786436
  3.1 9.0 %copy-start.4 = (f32[2,4,8,512]{3,2,1,0:T(8,128)S(1)}, f32[2,4,8,512]{3,2,1,0:T(8,128)}, u32[]{:S(2)}) copy-start(f32[2,4,8,512]{3,2,1,0:T(8,128)} %refs_4_.3) | copy-start | bytes 393220
  5.6 13.6 %collective-permute-start = (f32[576,128]{1,0:T(8,128)S(1)}, f32[576,128]{1,0:T(8,128)S(1)}, u32[]{:S(2)}, u32[]{:S(2)}) collective-permute-start(f32[576,128]{1,0:T(8,128)S(1)} %get-tuple-element.17), channel_id=1, source_target_pairs={{0,1},{1,2},{2,3},{3,4},{4,5},{5,6},{6,7},{7,8},{8,9},{9,10},{10,1... | collective-permute-start | bytes 884744 | tf_op jit(solution)/shard_map/ppermute | solution.py:436
  6.1 13.1 %collective-permute-start.1 = (f32[576,128]{1,0:T(8,128)S(1)}, f32[576,128]{1,0:T(8,128)S(1)}, u32[]{:S(2)}, u32[]{:S(2)}) collective-permute-start(f32[576,128]{1,0:T(8,128)S(1)} %get-tuple-element.18), channel_id=1, source_target_pairs={{1,0},{2,1},{3,2},{4,3},{5,4},{6,5},{7,6},{8,7},{9,8},{10,9},{11,1... | collective-permute-start | bytes 884744 | tf_op jit(solution)/shard_map/ppermute | solution.py:437
  12.1 1.4 %copy-start.2 = (bf16[3,512,512]{2,1,0:T(8,128)(2,1)S(1)}, bf16[3,512,512]{2,1,0:T(8,128)(2,1)}, u32[]{:S(2)}) copy-start(bf16[3,512,512]{2,1,0:T(8,128)(2,1)} %constant.4.clone.refs_0_) | copy-start | bytes 4718596
  13.5 0.9 %copy-start.5 = (f32[2,4,8,512]{3,2,1,0:T(8,128)S(1)}, f32[2,4,8,512]{3,2,1,0:T(8,128)}, u32[]{:S(2)}) copy-start(f32[2,4,8,512]{3,2,1,0:T(8,128)} %refs_5_.3) | copy-start | bytes 393220
  14.4 4.8 %copy-start.8 = (s32[2,512]{1,0:T(2,128)S(1)}, s32[2,512]{1,0:T(2,128)}, u32[]{:S(2)}) copy-start(s32[2,512]{1,0:T(2,128)} %refs_11_.1) | copy-start | bytes 12292
  14.4 4.8 %copy-start.9 = (s32[512,1]{0,1:T(1,128)S(1)}, s32[512,1]{0,1:T(1,128)}, u32[]{:S(2)}) copy-start(s32[512,1]{0,1:T(1,128)} %param.17) | copy-start | bytes 6148
  14.4 4.8 %copy-start.10 = (s32[512]{0:T(512)S(1)}, s32[512]{0:T(512)}, u32[]{:S(2)}) copy-start(s32[512]{0:T(512)} %param.18) | copy-start | bytes 6148
  14.4 4.8 %copy-start.11 = (s32[32]{0:T(128)S(1)}, s32[32]{0:T(128)}, u32[]{:S(2)}) copy-start(s32[32]{0:T(128)} %param.19) | copy-start | bytes 388

commit v3 on v2

--- a/solution.py
+++ b/solution.py
@@ -128,44 +128,21 @@
     return jnp.take_along_axis(values, index, axis=1, mode="promise_in_bounds")
 
 
-def rim_kernel(last, faces_hbm, vel_hbm, sizes_hbm, lo_first, hi_first, lo_last, hi_last, faces, vel, sizes, made, sems):
-    tiles = ((last, (lo_last, hi_last)), (0, (lo_first, hi_first)))
-    copies = []
-
-    def begin(source, target):
-        copy = pltpu.make_async_copy(source, target, sems.at[len(copies)])
-        copy.start()
-        copies.append(copy)
-        return copy
-
-    waits = [begin(faces_hbm, faces)]
-    for n, (l, _) in enumerate(tiles):
-        columns = pl.ds(l * CROSS, CROSS)
-        waits.append(begin(vel_hbm.at[:, :, columns], vel.at[n]))
-        waits.append(begin(sizes_hbm.at[:, columns], sizes.at[n]))
+def rim_kernel(last, faces, vel, sizes, lo_first, hi_last):
     sub = iota((64, CROSS), 0) % 8
     before, after = span_lanes(EZN - 1), span_lanes(1)
-    waits[0].wait()
-    results = []
-    for n, (l, outs) in enumerate(tiles):
-        waits[1 + 2 * n].wait()
-        waits[2 + 2 * n].wait()
+    for face, l, out in ((1, last, hi_last), (0, 0, lo_first)):
+        lanes = slice(l * CROSS, (l + 1) * CROSS)
         for c in range(3):
-            products = dot(faces[...], vel[n, c])
-            for face in range(2):
-                for a in range(3):
-                    at = (face * 3 + a) * 64
-                    part = products[at : at + 64] * sizes[n, a : a + 1, :]
-                    low, high = normal_sums(part[:8], part[56:])
-                    part = jnp.concatenate([low, part[8:56], high], axis=0)
-                    swapped = jnp.where(sub == 0, moved(part, after), moved(part, before))
-                    swapped = pltpu.roll(swapped.reshape(8, 8, CROSS), 4, 1).reshape(64, CROSS)
-                    part = part + jnp.where((sub == 0) | (sub == 4), swapped, 0.0)
-                    made[n, face, pl.ds((c * 3 + a) * 64, 64), :] = part
-        for face in range(2):
-            results.append(begin(made.at[n, face], outs[face]))
-    for copy in results:
-        copy.wait()
+            products = dot(faces[face * 192 : face * 192 + 192, :], vel[c, :, lanes])
+            for a in range(3):
+                part = products[a * 64 : a * 64 + 64] * sizes[a : a + 1, lanes]
+                low, high = normal_sums(part[:8], part[56:])
+                part = jnp.concatenate([low, part[8:56], high], axis=0)
+                swapped = jnp.where(sub == 0, moved(part, after), moved(part, before))
+                swapped = pltpu.roll(swapped.reshape(8, 8, CROSS), 4, 1).reshape(64, CROSS)
+                part = part + jnp.where((sub == 0) | (sub == 4), swapped, 0.0)
+                out[pl.ds((c * 3 + a) * 64, 64), :] = part
 
 
 def routes(devices, capacity, pt_ref, brick_ref, block_ref, home_ref):
@@ -226,23 +203,52 @@
     return jnp.where(halfdet < 0.0, q + turn, q - turn)
 
 
-def layer_pieces(layers, arrays, waits, belows, aboves, part, lam, along, store, before_stitch):
-    op, vel, sizes, rx, ry, rz = arrays
-    count = len(layers)
-    lanes = [slice(l * CROSS, (l + 1) * CROSS) for l in layers]
-
-    def joined(read):
-        if layers[-1] - layers[0] == count - 1:
-            return read(slice(lanes[0].start, lanes[-1].stop))
-        return jnp.concatenate([read(at) for at in lanes], axis=1)
-
+def resample_layer(lam, l, lanes, rx, ry, rz, along, store, at):
+    for o in range(2):
+        for j in range(8):
+            rows = [lam[l, pl.ds((j * 8 + k) * 8, 8), :] for k in range(8)]
+            for w in range(4):
+                total = rows[0] * rz[o, w, ORDER[0] : ORDER[0] + 1, lanes]
+                for k in range(1, 8):
+                    total = total + rows[k] * rz[o, w, ORDER[k] : ORDER[k] + 1, lanes]
+                along[0, pl.ds((w * 8 + j) * 8, 8), :] = total
+        for w in range(4):
+            rows = [along[0, pl.ds((w * 8 + j) * 8, 8), :] for j in range(8)]
+            for v in range(4):
+                total = rows[0] * ry[o, v, 0:1, lanes]
+                for j in range(1, 8):
+                    total = total + rows[j] * ry[o, v, j : j + 1, lanes]
+                along[1, pl.ds((v * 4 + w) * 8, 8), :] = total
+        rows = [along[1, pl.ds(i, 16, stride=8), :] for i in range(8)]
+        for u in range(8):
+            total = rows[0] * rx[o, u, ORDER[0] : ORDER[0] + 1, lanes]
+            for i in range(1, 8):
+                total = total + rows[i] * rx[o, u, ORDER[i] : ORDER[i] + 1, lanes]
+            high, low = halves_of(total)
+            columns = pl.ds((at * 2 + o) * CROSS, CROSS)
+            store[pl.ds(u * 16, 16), columns] = high
+            store[pl.ds(128 + u * 16, 16), columns] = low
+
+
+def started(pairs, sems):
+    copies = [pltpu.make_async_copy(source, target, sems.at[n]) for n, (source, target) in enumerate(pairs)]
+    for copy in copies:
+        copy.start()
+    return copies
+
+
+def layer_lanes(l):
+    return slice(l * CROSS, (l + 1) * CROSS)
+
+
+def inner_kernel(layers, op, vel, sizes, rx, ry, rz, store, lam_ends, lo_first, hi_last, part, lam, along):
+    last = layers - 1
     before, after = span_lanes(EZN - 1), span_lanes(1)
     for c in range(3):
-        velocities = joined(lambda at: vel[c, :, at])
         for a in range(3):
-            products = dot(op[a], velocities) * joined(lambda at: sizes[a : a + 1, at])
-            for l in range(count):
-                values = products[:, l * CROSS : (l + 1) * CROSS]
+            products = dot(op[a], vel[c]) * sizes[a : a + 1, :]
+            for l in range(layers):
+                values = products[:, layer_lanes(l)]
                 first, final = normal_sums(values[:64], values[448:])
                 for j in range(8):
                     rows = {0: first, 7: final}.get(j, values[j * 64 : (j + 1) * 64])
@@ -252,88 +258,48 @@
                     part[l, pl.ds(at + 8, 24), :] = rows[8:32]
                     part[l, pl.ds(at + 32, 8), :] = far + moved(near, after)
                     part[l, pl.ds(at + 40, 24), :] = rows[40:]
-    before_stitch()
+
+    def face_sums(ca, carry):
+        near, far = pl.ds(ca * 512, 64, stride=8), pl.ds(ca * 512 + 4, 64, stride=8)
+        for l in range(last):
+            shared = part[l, far, :] + part[l + 1, near, :]
+            part[l, far, :] = shared
+            part[l + 1, near, :] = shared
+        rows = pl.ds(ca * 64, 64)
+        lo_first[rows, :] = part[0, near, :]
+        hi_last[rows, :] = part[last, far, :]
+        return carry
+
+    lax.fori_loop(0, 9, face_sums, 0, unroll=3)
+
+    def eigen(l, target, n):
+        def point_row(jk, carry):
+            g = [part[l, pl.ds(ca * 512 + jk * 8, 8), :] for ca in range(9)]
+            target[n, pl.ds(jk * 8, 8), :] = middle_eigen([g[0:3], g[3:6], g[6:9]])
+            return carry
+
+        lax.fori_loop(0, 64, point_row, 0, unroll=16)
+
+    for l in range(layers):
+        if l in (0, last):
+            eigen(l, lam_ends, min(l, 1))
+        else:
+            eigen(l, lam, 0)
+            resample_layer(lam, 0, layer_lanes(l), rx, ry, rz, along, store, l - 1)
+
+
+def outer_kernel(last, devices, capacity, *refs):
+    (rx, ry, rz, lam_ends, lo_first, hi_last, inner), hbm, send_hbm = refs[:7], refs[7:13], refs[13]
+    local, (lam, along, store, send, sems) = refs[14:20], refs[20:]
+    waits = started(list(zip(hbm, local)), sems)
+    lam[...] = lam_ends[...]
     for copy in waits:
         copy.wait()
-
-    def face_sums(ca, carry):
-        near, far = pl.ds(ca * 512, 64, stride=8), pl.ds(ca * 512 + 4, 64, stride=8)
-        rows = pl.ds(ca * 64, 64)
-        for l in range(count):
-            if belows[l] is not None:
-                part[l, near, :] = part[l, near, :] + belows[l][rows, :]
-            if aboves[l] is not None:
-                part[l, far, :] = part[l, far, :] + aboves[l][rows, :]
-            else:
-                shared = part[l, far, :] + part[l + 1, near, :]
-                part[l, far, :] = shared
-                part[l + 1, near, :] = shared
-        return carry
-
-    lax.fori_loop(0, 9, face_sums, 0, unroll=3)
-
-    def point_row(jk, l):
-        g = [part[l, pl.ds(ca * 512 + jk * 8, 8), :] for ca in range(9)]
-        lam[pl.ds(jk * 8, 8), :] = middle_eigen([g[0:3], g[3:6], g[6:9]])
-
-    for l in range(count):
-        lax.fori_loop(0, 64, lambda jk, carry, l=l: (point_row(jk, l), carry)[1], 0, unroll=16)
-        cols = lanes[l]
-        for o in range(2):
-            for j in range(8):
-                rows = [lam[pl.ds((j * 8 + k) * 8, 8), :] for k in range(8)]
-                for w in range(4):
-                    total = rows[0] * rz[o, w, ORDER[0] : ORDER[0] + 1, cols]
-                    for k in range(1, 8):
-                        total = total + rows[k] * rz[o, w, ORDER[k] : ORDER[k] + 1, cols]
-                    along[0, pl.ds((w * 8 + j) * 8, 8), :] = total
-            for w in range(4):
-                rows = [along[0, pl.ds((w * 8 + j) * 8, 8), :] for j in range(8)]
-                for v in range(4):
-                    total = rows[0] * ry[o, v, 0:1, cols]
-                    for j in range(1, 8):
-                        total = total + rows[j] * ry[o, v, j : j + 1, cols]
-                    along[1, pl.ds((v * 4 + w) * 8, 8), :] = total
-            rows = [along[1, pl.ds(i, 16, stride=8), :] for i in range(8)]
-            for u in range(8):
-                total = rows[0] * rx[o, u, ORDER[0] : ORDER[0] + 1, cols]
-                for i in range(1, 8):
-                    total = total + rows[i] * rx[o, u, ORDER[i] : ORDER[i] + 1, cols]
-                high, low = halves_of(total)
-                columns = pl.ds((l * 2 + o) * CROSS, CROSS)
-                store[pl.ds(u * 16, 16), columns] = high
-                store[pl.ds(128 + u * 16, 16), columns] = low
-
-
-def started(pairs, sems):
-    copies = [pltpu.make_async_copy(source, target, sems.at[n]) for n, (source, target) in enumerate(pairs)]
-    for copy in copies:
-        copy.start()
-    return copies
-
-
-def inner_kernel(layers, *refs):
-    arrays, (below_hbm, above_hbm, store, lo_out, hi_out, below, above, part, lam, along, sems) = refs[:6], refs[6:]
-    count = len(layers)
-    waits = started([(below_hbm, below), (above_hbm, above)], sems)
-
-    def give_faces():
-        lo_out[...] = part[0, pl.ds(0, 576, stride=8), :]
-        hi_out[...] = part[count - 1, pl.ds(4, 576, stride=8), :]
-
-    belows = [below] + [None] * (count - 1)
-    aboves = [None] * (count - 1) + [above]
-    layer_pieces(layers, arrays, waits, belows, aboves, part, lam, along, store, give_faces)
-
-
-def outer_kernel(last, devices, capacity, *refs):
-    arrays, (above_first, below_last, inner), hbm, send_hbm = refs[:6], refs[6:9], refs[9:15], refs[15]
-    local, (part, lam, along, store, send, sems) = refs[16:22], refs[22:]
-    waits = started(list(zip(hbm, local)), sems)
-    below_first, above_last = local[:2]
-    layer_pieces(
-        (0, last), arrays, waits, [below_first, below_last], [above_first, above_last], part, lam, along, store, lambda: None
-    )
+    for n, own, other, at in ((0, lo_first, local[0], 0), (1, hi_last, local[1], 4)):
+        g = [own[ca * 64 : ca * 64 + 64, :] + other[ca * 64 : ca * 64 + 64, :] for ca in range(9)]
+        lam[n, pl.ds(at, 64, stride=8), :] = middle_eigen([g[0:3], g[3:6], g[6:9]])
+    for n, l in ((0, 0), (1, last)):
+        resample_layer(lam, n, layer_lanes(l), rx, ry, rz, along, store, n)
     slots, ids = routes(devices, capacity, *local[2:])
     numbers = jnp.concatenate(halves_of(ids), axis=1)
     total = send.shape[0]
@@ -344,9 +310,7 @@
         rows = iota((size, CROSS), 0) + n * size
 
         def chosen(which):
-            return jnp.concatenate(
-                [onehot(rows == slots[o][:, l * CROSS : (l + 1) * CROSS]) for l in which for o in range(2)], axis=1
-            )
+            return jnp.concatenate([onehot(rows == slots[o][:, layer_lanes(l)]) for l in which for o in range(2)], axis=1)
 
         homes = iota((size, devices), 1) * (capacity + 1) + capacity
         numbered = onehot(iota((size, devices), 0) + n * size == homes)
@@ -391,8 +355,14 @@
         copy.wait()
 
 
-def params():
-    return pltpu.CompilerParams(vmem_limit_bytes=24 * 1024 * 1024)
+def kernel_call(kernel, name, micros, megabytes=24, **rest):
+    return pl.pallas_call(
+        kernel,
+        name=name,
+        cost_estimate=pl.CostEstimate(flops=int(micros * 1e9), bytes_accessed=0, transcendentals=0),
+        compiler_params=pltpu.CompilerParams(vmem_limit_bytes=megabytes * 1024 * 1024),
+        **rest,
+    )
 
 
 FAR = pl.BlockSpec(memory_space=pltpu.HBM)
@@ -415,46 +385,37 @@
     devices = lax.axis_size("dom")
     capacity = max(2, 4 * elements // devices)
     whole, faces = (jnp.asarray(o) for o in operators())
+    layers = last + 1
     face = (576, CROSS)
     face_shape = jax.ShapeDtypeStruct(face, F32)
-
-    lo_first, hi_first, lo_last, hi_last = pl.pallas_call(
+    ends_shape = jax.ShapeDtypeStruct((2, 512, CROSS), F32)
+
+    rim_lo, rim_hi = kernel_call(
         functools.partial(rim_kernel, last),
-        in_specs=[FAR] * 3,
-        out_specs=[FAR] * 4,
-        out_shape=[face_shape] * 4,
+        "rim_faces",
+        3,
+        in_specs=[NEAR] * 3,
+        out_specs=[NEAR] * 2,
+        out_shape=[face_shape] * 2,
+    )(faces, velocity, inverse_sizes)
+    from_prev = lax.ppermute(rim_hi, "dom", [(i, (i + 1) % devices) for i in range(devices)])
+    from_next = lax.ppermute(rim_lo, "dom", [((i + 1) % devices, i) for i in range(devices)])
+
+    weights = (resample_x, resample_y, resample_z)
+    along = pltpu.VMEM((2, 256, CROSS), F32)
+    inner, lam_ends, lo_first, hi_last = kernel_call(
+        functools.partial(inner_kernel, layers),
+        "inner_layers",
+        9,
+        in_specs=[NEAR] * 6,
+        out_specs=[NEAR] * 4,
+        out_shape=[jax.ShapeDtypeStruct((256, (layers - 2) * 256), BF16), ends_shape, face_shape, face_shape],
         scratch_shapes=[
-            pltpu.VMEM(faces.shape, BF16),
-            pltpu.VMEM((2, 3, 512, CROSS), BF16),
-            pltpu.VMEM((2, 3, CROSS), F32),
-            pltpu.VMEM((2, 2) + face, F32),
-            pltpu.SemaphoreType.DMA((9,)),
+            pltpu.VMEM((layers, 4608, CROSS), F32),
+            pltpu.VMEM((1, 512, CROSS), F32),
+            along,
         ],
-        compiler_params=params(),
-        name="rim_faces",
-    )(faces, velocity, inverse_sizes)
-    from_prev = lax.ppermute(hi_last, "dom", [(i, (i + 1) % devices) for i in range(devices)])
-    from_next = lax.ppermute(lo_first, "dom", [((i + 1) % devices, i) for i in range(devices)])
-
-    arrays = (whole, velocity, inverse_sizes, resample_x, resample_y, resample_z)
-
-    def scratch(count):
-        return [
-            pltpu.VMEM((count, 4608, CROSS), F32),
-            pltpu.VMEM((512, CROSS), F32),
-            pltpu.VMEM((2, 256, CROSS), F32),
-        ]
-
-    inside = tuple(range(1, last))
-    inner, lo_inner, hi_inner = pl.pallas_call(
-        functools.partial(inner_kernel, inside),
-        in_specs=[NEAR] * 6 + [FAR] * 2,
-        out_specs=[NEAR] * 3,
-        out_shape=[jax.ShapeDtypeStruct((256, len(inside) * 256), BF16), face_shape, face_shape],
-        scratch_shapes=[pltpu.VMEM(face, F32)] * 2 + scratch(len(inside)) + [pltpu.SemaphoreType.DMA((2,))],
-        compiler_params=params(),
-        name="inner_layers",
-    )(*arrays, hi_first, lo_last)
+    )(whole, velocity, inverse_sizes, *weights)
 
     rows = devices * (capacity + 1)
     routing = (
@@ -463,25 +424,32 @@
         target_block.reshape(1, elements),
         brick_home.reshape(1, -1),
     )
-    sendbuf = pl.pallas_call(
+    sendbuf = kernel_call(
         functools.partial(outer_kernel, last, devices, capacity),
-        in_specs=[NEAR] * 9 + [FAR] * 6,
+        "outer_layers",
+        5,
+        in_specs=[NEAR] * 7 + [FAR] * 6,
         out_specs=FAR,
         out_shape=jax.ShapeDtypeStruct((rows, 128), F32),
         scratch_shapes=[pltpu.VMEM(face, F32)] * 2
         + [pltpu.VMEM(array.shape, array.dtype) for array in routing]
-        + scratch(2)
-        + [pltpu.VMEM((256, 512), BF16), pltpu.VMEM((rows, 128), F32), pltpu.SemaphoreType.DMA((10,))],
-        compiler_params=params(),
-        name="outer_layers",
-    )(*arrays, lo_inner, hi_inner, inner, from_prev, from_next, *routing)
+        + [
+            pltpu.VMEM(ends_shape.shape, F32),
+            along,
+            pltpu.VMEM((256, 512), BF16),
+            pltpu.VMEM((rows, 128), F32),
+            pltpu.SemaphoreType.DMA((10,)),
+        ],
+    )(*weights, lam_ends, lo_first, hi_last, inner, from_prev, from_next, *routing)
 
     received = lax.all_to_all(
         sendbuf.reshape(devices, 1, (capacity + 1) * 128), "dom", split_axis=0, concat_axis=0, tiled=True
     )
     wide = -(-rows // 128) * 128
-    image = pl.pallas_call(
+    image = kernel_call(
         functools.partial(gather_kernel, devices, capacity),
+        "block_sums",
+        4,
         in_specs=[NEAR],
         out_specs=FAR,
         out_shape=jax.ShapeDtypeStruct((BLOCKS, 128), F32),
@@ -491,8 +459,6 @@
             pltpu.VMEM((BLOCKS, 128), F32),
             pltpu.SemaphoreType.DMA((8,)),
         ],
-        compiler_params=params(),
-        name="block_sums",
     )(received.reshape(rows, 128))
     return image[None]
 

time: 63.5 us -> 58.5 us (0.921)
  local copies, waits for them, and re-layouts: 5.43 us -> 3.14 us
  Pallas kernels: 19.9 us -> 17.7 us
    unnamed x24, local copies, waits for them, and re-layouts: 5.43 us -> 3.14 us
    pallas_call x4, Pallas kernels: 19.9 us -> 17.7 us  [the longest x1 7.91 us: shards(): kernel_call(functools.partial(inner_kernel, layers), 'inner_layers', 9, i...]
  transfers between devices with their start and end apart: 2 -> 2, of which waited for: 0 -> 0; matrix products, arithmetic and copies ran while one was open for 0% -> 0% of each run, Pallas kernels for 8% -> 14%
where the time goes in v3:
time: 58.5 us; the launch traced here: 58.3 us
  blocking collectives  30.8 us (53%)
  Pallas kernels  17.7 us (30%)
  starting transfers between devices  6.51 us (11%)
  local copies, waits for them, and re-layouts  3.14 us (5%)
    all_to_all x1, blocking collectives, shards(): lax.all_to_all(sendbuf.reshape(devices, 1, (capacity + 1) * 128), 'dom',...  30.8 us
    pallas_call x1, Pallas kernels, shards(): kernel_call(functools.partial(inner_kernel, layers), 'inner_layers', 9, i...  7.91 us
    ppermute x1, starting transfers between devices, shards(): lax.ppermute(rim_lo, 'dom', [((i + 1) % devices, i) for i in range(device...  6.02 us
    pallas_call x1, Pallas kernels, shards(): kernel_call(functools.partial(outer_kernel, last, devices, capacity), 'ou...  5.07 us
    pallas_call x1, Pallas kernels, shards(): kernel_call(functools.partial(gather_kernel, devices, capacity), 'block_s...  3.75 us
    unnamed x24, local copies, waits for them, and re-layouts  3.14 us
  transfers between devices with their start and end apart: 2, of which 0 were waited for; matrix products, arithmetic and copies ran while one was open for 0% of the time, Pallas kernels for 14%

profile of v3, /device:TPU:0, one launch (start us, length us, event | category | flops | bytes accessed | tf_op | source)
XLA Modules:
  0.0 58.3 jit_solution(2971456179654051115)
XLA Ops:
  0.0 0.0 copy-start
  0.0 1.4 %copy-done = bf16[3,512,512]{2,1,0:T(8,128)(2,1)S(1)} copy-done((bf16[3,512,512]{2,1,0:T(8,128)(2,1)S(1)}, bf16[3,512,512]{2,1,0:T(8,128)(2,1)}, u32[]{:S(2)}) %copy-start) | copy-done | bytes 1572888
  1.4 0.0 copy-start.5
  1.4 0.7 %copy-done.5 = f32[3,512]{1,0:T(4,128)S(1)} copy-done((f32[3,512]{1,0:T(4,128)S(1)}, f32[3,512]{1,0:T(4,128)}, u32[]{:S(2)}) %copy-start.5) | copy-done | bytes 6168
  2.1 0.0 copy-start.11
  2.1 1.0 %copy-done.11 = bf16[384,512]{1,0:T(8,128)(2,1)S(1)} copy-done((bf16[384,512]{1,0:T(8,128)(2,1)S(1)}, bf16[384,512]{1,0:T(8,128)(2,1)}, u32[]{:S(2)}) %copy-start.11) | copy-done | bytes 393240
  3.1 0.0 copy-start.1
  3.1 0.0 copy-start.2
  3.1 0.0 copy-start.3
  3.1 0.0 copy-start.4
  3.1 0.0 copy-start.10
  3.1 1.0 %rim_faces.1 = (f32[576,128]{1,0:T(8,128)S(1)}, f32[576,128]{1,0:T(8,128)S(1)}) custom-call(bf16[384,512]{1,0:T(8,128)(2,1)S(1)} %copy-done.11, bf16[3,512,512]{2,1,0:T(8,128)(2,1)S(1)} %copy-done, f32[3,512]{1,0:T(4,128)S(1)} %copy-done.5), custom_call_target="tpu_custom_call" | custom-call | flops 3000000000 | tf_op jit(solution)/shard_map/rim_faces/pallas_call | solution.py:393
  4.1 0.5 collective-permute-start
  4.6 0.0 copy-start.6
  4.6 0.0 copy-start.8
  4.6 0.0 copy-start.9
  4.6 6.0 %collective-permute-start.1 = (f32[576,128]{1,0:T(8,128)S(1)}, f32[576,128]{1,0:T(8,128)S(1)}, u32[]{:S(2)}, u32[]{:S(2)}) collective-permute-start(f32[576,128]{1,0:T(8,128)S(1)} %get-tuple-element.16), channel_id=1, source_target_pairs={{1,0},{2,1},{3,2},{4,3},{5,4},{6,5},{7,6},{8,7},{9,8},{10,9},{11,1... | collective-permute-start | bytes 884744 | tf_op jit(solution)/shard_map/ppermute | solution.py:402
  10.6 0.0 copy-done.1
  10.6 0.0 copy-done.2
  10.6 0.0 copy-done.3
  10.6 0.0 copy-done.4
  10.6 0.0 copy-done.10
  10.6 7.9 %inner_layers.1 = (bf16[256,512]{1,0:T(8,128)(2,1)S(1)}, f32[2,512,128]{2,1,0:T(8,128)S(1)}, f32[576,128]{1,0:T(8,128)S(1)}, f32[576,128]{1,0:T(8,128)S(1)}) custom-call(bf16[3,512,512]{2,1,0:T(8,128)(2,1)S(1)} %copy-done.10, bf16[3,512,512]{2,1,0:T(8,128)(2,1)S(1)} %copy-done.1, f32[3,512]{1,0:T(4,128)S(1)} %copy-done.5, f32[2,8,8,512]{3,2,1,0:T(8,128)S(1)} %copy-done.2, ...), custom_call_target="tpu_custom_call" | custom-call | flops 8999999488 | tf_op jit(solution)/shard_map/inner_layers/pallas_call | solution.py:406
  18.6 0.0 collective-permute-done.refs_7_
  18.6 0.0 collective-permute-done.1.refs_8_
  18.6 0.0 copy-done.6
  18.6 0.0 copy-done.7
  18.6 0.0 copy-done.8
  18.6 0.0 copy-done.9
  18.6 5.1 %outer_layers.1 = f32[2080,128]{1,0:T(8,128)S(1)} custom-call(f32[2,8,8,512]{3,2,1,0:T(8,128)S(1)} %copy-done.2, f32[2,4,8,512]{3,2,1,0:T(8,128)S(1)} %copy-done.3, f32[2,4,8,512]{3,2,1,0:T(8,128)S(1)} %copy-done.4, f32[2,512,128]{2,1,0:T(8,128)S(1)} %get-tuple-element.11.refs_3_, f32[576,128]{1,0:T(8,128)S(1)} %get-tuple-element.12.refs_4_, ...), custom_call_target="tpu_custom_call" | custom-call | flops 5000000000 | tf_op jit(solution)/shard_map/outer_layers/pallas_call | solution.py:427
  23.7 30.8 %all_to_all.5 = f32[32,1,8320]{2,1,0:T(1,128)S(1)} all-to-all(f32[32,1,8320]{2,1,0:T(1,128)S(1)} %bitcast.6), channel_id=1, replica_groups=mesh['dom'=32] {'dom'}, dimensions={0} | all-to-all | bytes 2129920 | tf_op jit(solution)/shard_map/all_to_all | solution.py:445
  54.5 3.8 %block_sums.1 = f32[2048,128]{1,0:T(8,128)} custom-call(f32[2080,128]{1,0:T(8,128)S(1)} %bitcast.7), custom_call_target="tpu_custom_call" | custom-call | flops 4000000000 | tf_op jit(solution)/shard_map/block_sums/pallas_call | solution.py:449
  (1 shorter events, 0.0 us)
Async XLA Ops:
  0.0 1.4 %copy-start = (bf16[3,512,512]{2,1,0:T(8,128)(2,1)S(1)}, bf16[3,512,512]{2,1,0:T(8,128)(2,1)}, u32[]{:S(2)}) copy-start(bf16[3,512,512]{2,1,0:T(8,128)(2,1)} %vel.3) | copy-start | bytes 4718596
  1.4 0.7 %copy-start.5 = (f32[3,512]{1,0:T(4,128)S(1)}, f32[3,512]{1,0:T(4,128)}, u32[]{:S(2)}) copy-start(f32[3,512]{1,0:T(4,128)} %sizes.3) | copy-start | bytes 18436
  2.1 1.0 %copy-start.11 = (bf16[384,512]{1,0:T(8,128)(2,1)S(1)}, bf16[384,512]{1,0:T(8,128)(2,1)}, u32[]{:S(2)}) copy-start(bf16[384,512]{1,0:T(8,128)(2,1)} %constant.5.clone.faces) | copy-start | bytes 1179652
  3.1 7.5 %copy-start.1 = (bf16[3,512,512]{2,1,0:T(8,128)(2,1)S(1)}, bf16[3,512,512]{2,1,0:T(8,128)(2,1)}, u32[]{:S(2)}) copy-start(bf16[3,512,512]{2,1,0:T(8,128)(2,1)} %vel.3) | copy-start | bytes 4718596
  3.1 7.5 %copy-start.2 = (f32[2,8,8,512]{3,2,1,0:T(8,128)S(1)}, f32[2,8,8,512]{3,2,1,0:T(8,128)}, u32[]{:S(2)}) copy-start(f32[2,8,8,512]{3,2,1,0:T(8,128)} %refs_0_.1) | copy-start | bytes 786436
  3.1 7.5 %copy-start.3 = (f32[2,4,8,512]{3,2,1,0:T(8,128)S(1)}, f32[2,4,8,512]{3,2,1,0:T(8,128)}, u32[]{:S(2)}) copy-start(f32[2,4,8,512]{3,2,1,0:T(8,128)} %refs_1_.1) | copy-start | bytes 393220
  3.1 7.5 %copy-start.4 = (f32[2,4,8,512]{3,2,1,0:T(8,128)S(1)}, f32[2,4,8,512]{3,2,1,0:T(8,128)}, u32[]{:S(2)}) copy-start(f32[2,4,8,512]{3,2,1,0:T(8,128)} %refs_2_.1) | copy-start | bytes 393220
  3.1 7.5 %copy-start.10 = (bf16[3,512,512]{2,1,0:T(8,128)(2,1)S(1)}, bf16[3,512,512]{2,1,0:T(8,128)(2,1)}, u32[]{:S(2)}) copy-start(bf16[3,512,512]{2,1,0:T(8,128)(2,1)} %constant.4.clone.op) | copy-start | bytes 4718596
  4.1 14.5 %collective-permute-start = (f32[576,128]{1,0:T(8,128)S(1)}, f32[576,128]{1,0:T(8,128)S(1)}, u32[]{:S(2)}, u32[]{:S(2)}) collective-permute-start(f32[576,128]{1,0:T(8,128)S(1)} %get-tuple-element.15), channel_id=1, source_target_pairs={{0,1},{1,2},{2,3},{3,4},{4,5},{5,6},{6,7},{7,8},{8,9},{9,10},{10,1... | collective-permute-start | bytes 884744 | tf_op jit(solution)/shard_map/ppermute | solution.py:401
  4.6 14.0 %copy-start.6 = (s32[2,512]{1,0:T(2,128)S(1)}, s32[2,512]{1,0:T(2,128)}, u32[]{:S(2)}) copy-start(s32[2,512]{1,0:T(2,128)} %refs_9_.1) | copy-start | bytes 12292
  4.6 14.0 %copy-start.7 = (s32[512,1]{0,1:T(1,128)S(1)}, s32[512,1]{0,1:T(1,128)}, u32[]{:S(2)}) copy-start(s32[512,1]{0,1:T(1,128)} %param.17) | copy-start | bytes 6148
  4.6 14.0 %copy-start.8 = (s32[512]{0:T(512)S(1)}, s32[512]{0:T(512)}, u32[]{:S(2)}) copy-start(s32[512]{0:T(512)} %param.18) | copy-start | bytes 6148
  4.6 14.0 %copy-start.9 = (s32[32]{0:T(128)S(1)}, s32[32]{0:T(128)}, u32[]{:S(2)}) copy-start(s32[32]{0:T(128)} %param.19) | copy-start | bytes 388
  4.6 14.0 %collective-permute-start.1 = (f32[576,128]{1,0:T(8,128)S(1)}, f32[576,128]{1,0:T(8,128)S(1)}, u32[]{:S(2)}, u32[]{:S(2)}) collective-permute-start(f32[576,128]{1,0:T(8,128)S(1)} %get-tuple-element.16), channel_id=1, source_target_pairs={{1,0},{2,1},{3,2},{4,3},{5,4},{6,5},{7,6},{8,7},{9,8},{10,9},{11,1... | collective-permute-start | bytes 884744 | tf_op jit(solution)/shard_map/ppermute | solution.py:402

commit v4 on v3

--- a/solution.py
+++ b/solution.py
@@ -31,7 +31,7 @@
 ORDER = [0, 1, 2, 3, 7, 4, 5, 6]
 
 
-def derivative_operator():
+def derivative_matrix():
     barycentric = []
     for first in range(8):
         product_term = 1.0
@@ -54,34 +54,40 @@
         row_values[first] = -sum(row_values)
         matrix_rows.append(row_values)
     diff_matrix = np.array(matrix_rows)
-    identity = np.eye(8)
-    return np.concatenate(
+    return diff_matrix
+
+
+def rounded_matrix():
+    return derivative_matrix().astype(np.float32).astype(ml_dtypes.bfloat16).astype(np.float32)
+
+
+def operator_rows():
+    matrix, identity = rounded_matrix(), np.eye(8, dtype=np.float32)
+    whole = np.stack(
         [
-            np.kron(np.kron(diff_matrix, identity), identity),
-            np.kron(np.kron(identity, diff_matrix), identity),
-            np.kron(np.kron(identity, identity), diff_matrix),
-        ],
-        axis=0,
-    )
-
-
-def operators():
-    rounded = derivative_operator().astype(np.float32).astype(ml_dtypes.bfloat16).astype(np.float32)
+            np.kron(np.kron(matrix, identity), identity),
+            np.kron(np.kron(identity, matrix), identity),
+            np.kron(np.kron(identity, identity), matrix),
+        ]
+    )
     ends = np.ones(8, np.float32)
     ends[0] = ends[7] = 0.5
     halves = ends[:, None, None] * ends[None, :, None] * ends[None, None, :]
-    rows = rounded.reshape(3, 8, 8, 8, 512) * halves[None, :, :, :, None]
-    rows = rows.transpose(0, 2, 3, 1, 4)[:, :, ORDER]
-    whole = rows[:, :, :, ORDER].reshape(3, 512, 512)
-    faces = np.stack([rows[:, :, :, 0], rows[:, :, :, 7]]).reshape(384, 512)
-    return whole.astype(ml_dtypes.bfloat16), faces.astype(ml_dtypes.bfloat16)
+    rows = whole.reshape(3, 8, 8, 8, 512) * halves[None, :, :, :, None]
+    rows = rows.transpose(0, 2, 3, 1, 4)[:, :, :, ORDER].reshape(3, 512, 512)
+    split = rows[::2].reshape(2, 2, 256, 8, 2, 32)
+    blocks = np.stack([split[:, half, :, :, half, :].reshape(2, 256, 256) for half in range(2)], axis=1)
+    return rows[1].astype(ml_dtypes.bfloat16), blocks.astype(ml_dtypes.bfloat16)
+
+
+MATRIX = rounded_matrix()
 
 
 def third_angle():
     spots = (1.0 - np.cos(np.pi * (np.arange(4000) + 0.5) / 4000)) / 2
     values = np.sin(np.arcsin(1.0 - spots * spots) / 3.0)
-    fitted = np.polynomial.chebyshev.Chebyshev.fit(spots, values, 9, domain=[0, 1])
-    return [float(c) for c in fitted.convert(kind=np.polynomial.Polynomial).coef]
+    fitted = np.polynomial.chebyshev.Chebyshev.fit(spots, values, 8, domain=[0, 1])
+    return [2.0 / math.sqrt(3.0) * float(c) for c in fitted.convert(kind=np.polynomial.Polynomial).coef]
 
 
 THIRD = third_angle()
@@ -128,21 +134,43 @@
     return jnp.take_along_axis(values, index, axis=1, mode="promise_in_bounds")
 
 
-def rim_kernel(last, faces, vel, sizes, lo_first, hi_last):
-    sub = iota((64, CROSS), 0) % 8
+def rim_kernel(last, vel, sizes, lo_first, hi_last):
+    sub = iota((8, CROSS), 0)
     before, after = span_lanes(EZN - 1), span_lanes(1)
-    for face, l, out in ((1, last, hi_last), (0, 0, lo_first)):
-        lanes = slice(l * CROSS, (l + 1) * CROSS)
+    ends = jnp.where((sub == 0) | (sub == 7), 0.5, 1.0)
+    turned = []
+    for shift in range(8):
+        column = jnp.zeros((8, CROSS), F32)
+        for k in range(8):
+            column = jnp.where(sub == k, float(MATRIX[k, (k - shift) % 8]), column)
+        turned.append(column)
+    for end, l, out in ((7, last, hi_last), (0, 0, lo_first)):
+        lanes = layer_lanes(l)
         for c in range(3):
-            products = dot(faces[face * 192 : face * 192 + 192, :], vel[c, :, lanes])
-            for a in range(3):
-                part = products[a * 64 : a * 64 + 64] * sizes[a : a + 1, lanes]
-                low, high = normal_sums(part[:8], part[56:])
-                part = jnp.concatenate([low, part[8:56], high], axis=0)
-                swapped = jnp.where(sub == 0, moved(part, after), moved(part, before))
-                swapped = pltpu.roll(swapped.reshape(8, 8, CROSS), 4, 1).reshape(64, CROSS)
-                part = part + jnp.where((sub == 0) | (sub == 4), swapped, 0.0)
-                out[pl.ds((c * 3 + a) * 64, 64), :] = part
+            line = [vel[c, i * 64 : i * 64 + 64, lanes].astype(F32) for i in range(8)]
+            along_x = line[0] * float(MATRIX[end, 0])
+            for i in range(1, 8):
+                along_x = along_x + line[i] * float(MATRIX[end, i])
+            face = [line[end][j * 8 : j * 8 + 8] for j in range(8)]
+            along_y, along_z = [], []
+            for j in range(8):
+                total = face[0] * float(MATRIX[j, 0])
+                for other in range(1, 8):
+                    total = total + face[other] * float(MATRIX[j, other])
+                along_y.append(total)
+                total = face[j] * turned[0]
+                for shift in range(1, 8):
+                    total = total + pltpu.roll(face[j], shift, 0) * turned[shift]
+                along_z.append(total)
+            for a, rows in enumerate(([along_x[j * 8 : j * 8 + 8] for j in range(8)], along_y, along_z)):
+                scale = sizes[a : a + 1, lanes] * (0.5 * ends)
+                rows = [row * scale for row in rows]
+                rows[0], rows[7] = normal_sums(rows[0] * 0.5, rows[7] * 0.5)
+                for j in range(8):
+                    low = pltpu.roll(moved(rows[j], before), 1, 0)
+                    high = pltpu.roll(moved(rows[j], after), 7, 0)
+                    shared = rows[j] + jnp.where(sub == 0, low, jnp.where(sub == 7, high, 0.0))
+                    out[pl.ds(((c * 3 + a) * 8 + j) * 8, 8), :] = shared
 
 
 def routes(devices, capacity, pt_ref, brick_ref, block_ref, home_ref):
@@ -178,29 +206,25 @@
 def middle_eigen(g):
     s01, s02, s12 = g[0][1] + g[1][0], g[0][2] + g[2][0], g[1][2] + g[2][1]
     p01, p02, p12 = g[0][1] * g[1][0], g[0][2] * g[2][0], g[1][2] * g[2][1]
-    m00 = g[0][0] * g[0][0] + (p01 + p02)
-    m11 = g[1][1] * g[1][1] + (p01 + p12)
-    m22 = g[2][2] * g[2][2] + (p02 + p12)
-    m01 = 0.5 * ((g[0][0] + g[1][1]) * s01 + (g[0][2] * g[2][1] + g[1][2] * g[2][0]))
-    m02 = 0.5 * ((g[0][0] + g[2][2]) * s02 + (g[0][1] * g[1][2] + g[2][1] * g[1][0]))
-    m12 = 0.5 * ((g[1][1] + g[2][2]) * s12 + (g[1][0] * g[0][2] + g[2][0] * g[0][1]))
-    q = (m00 + m11 + m22) * (1.0 / 3.0)
-    x, y, z = m00 - q, m11 - q, m22 - q
-    n01, n02, n12 = m01 * m01, m02 * m02, m12 * m12
-    spread = (x * x + y * y + z * z + 2.0 * (n01 + n02 + n12)) * (1.0 / 6.0)
-    halfdet = 0.5 * (x * (y * z - n12) - z * n01 - y * n02) + m01 * m02 * m12
+    d0, d1, d2 = g[0][0] * g[0][0] - p12, g[1][1] * g[1][1] - p02, g[2][2] * g[2][2] - p01
+    mean = (d0 + d1 + d2) * (1.0 / 3.0)
+    x, y, z = d0 - mean, d1 - mean, d2 - mean
+    q = mean + (p01 + p02 + p12)
+    o01 = (g[0][0] + g[1][1]) * s01 + (g[0][2] * g[2][1] + g[1][2] * g[2][0])
+    o02 = (g[0][0] + g[2][2]) * s02 + (g[0][1] * g[1][2] + g[2][1] * g[1][0])
+    o12 = (g[1][1] + g[2][2]) * s12 + (g[1][0] * g[0][2] + g[2][0] * g[0][1])
+    n01, n02, n12 = o01 * o01, o02 * o02, o12 * o12
+    spread = (y * y - x * z) + 0.25 * (n01 + n02 + n12)
+    det = 4.0 * (x * y * z) + (o01 * o02 * o12 - (x * n12 + z * n01 + y * n02))
     inverse = lax.rsqrt(jnp.maximum(spread, 1e-37))
-    ratio = ((jnp.abs(halfdet) * inverse) * inverse) * inverse
+    ratio = ((jnp.abs(det) * inverse) * inverse) * (inverse * (3.0 * math.sqrt(3.0) / 8.0))
     gap = jnp.maximum(1.0 - ratio, 1e-30)
     root = gap * lax.rsqrt(gap)
-    pairs = [THIRD[n] + THIRD[n + 1] * root for n in range(0, 10, 2)]
-    square = root * root
-    fourth = square * square
-    third = (pairs[0] + pairs[1] * square) + fourth * (
-        (pairs[2] + pairs[3] * square) + fourth * pairs[4]
-    )
-    turn = 2.0 * (spread * inverse) * third
-    return jnp.where(halfdet < 0.0, q + turn, q - turn)
+    third = THIRD[-1]
+    for coefficient in THIRD[-2::-1]:
+        third = third * root + coefficient
+    turn = (spread * inverse) * third
+    return jnp.where(det < 0.0, q + turn, q - turn)
 
 
 def resample_layer(lam, l, lanes, rx, ry, rz, along, store, at):
@@ -208,9 +232,9 @@
         for j in range(8):
             rows = [lam[l, pl.ds((j * 8 + k) * 8, 8), :] for k in range(8)]
             for w in range(4):
-                total = rows[0] * rz[o, w, ORDER[0] : ORDER[0] + 1, lanes]
+                total = rows[0] * rz[o, w, 0:1, lanes]
                 for k in range(1, 8):
-                    total = total + rows[k] * rz[o, w, ORDER[k] : ORDER[k] + 1, lanes]
+                    total = total + rows[k] * rz[o, w, k : k + 1, lanes]
                 along[0, pl.ds((w * 8 + j) * 8, 8), :] = total
         for w in range(4):
             rows = [along[0, pl.ds((w * 8 + j) * 8, 8), :] for j in range(8)]
@@ -241,23 +265,30 @@
     return slice(l * CROSS, (l + 1) * CROSS)
 
 
-def inner_kernel(layers, op, vel, sizes, rx, ry, rz, store, lam_ends, lo_first, hi_last, part, lam, along):
+def inner_kernel(layers, across, blocks, vel, sizes, rx, ry, rz, store, lam_ends, lo_first, hi_last, part, lam, along):
     last = layers - 1
     before, after = span_lanes(EZN - 1), span_lanes(1)
     for c in range(3):
+        halves = [
+            jnp.concatenate([vel[c, i * 64 + half * 32 : i * 64 + half * 32 + 32, :] for i in range(8)], axis=0)
+            for half in range(2)
+        ]
         for a in range(3):
-            products = dot(op[a], vel[c]) * sizes[a : a + 1, :]
+            if a == 1:
+                products = dot(across[...], vel[c])
+            else:
+                products = jnp.concatenate([dot(blocks[a // 2, half], halves[half]) for half in range(2)], axis=0)
+            products = products * sizes[a : a + 1, :]
             for l in range(layers):
                 values = products[:, layer_lanes(l)]
                 first, final = normal_sums(values[:64], values[448:])
                 for j in range(8):
                     rows = {0: first, 7: final}.get(j, values[j * 64 : (j + 1) * 64])
-                    near, far = rows[:8], rows[32:40]
+                    near, far = rows[:8], rows[56:]
                     at = (c * 3 + a) * 512 + j * 64
                     part[l, pl.ds(at, 8), :] = near + moved(far, before)
-                    part[l, pl.ds(at + 8, 24), :] = rows[8:32]
-                    part[l, pl.ds(at + 32, 8), :] = far + moved(near, after)
-                    part[l, pl.ds(at + 40, 24), :] = rows[40:]
+                    part[l, pl.ds(at + 8, 48), :] = rows[8:56]
+                    part[l, pl.ds(at + 56, 8), :] = far + moved(near, after)
 
     def face_sums(ca, carry):
         near, far = pl.ds(ca * 512, 64, stride=8), pl.ds(ca * 512 + 4, 64, stride=8)
@@ -273,12 +304,9 @@
     lax.fori_loop(0, 9, face_sums, 0, unroll=3)
 
     def eigen(l, target, n):
-        def point_row(jk, carry):
+        for jk in range(64):
             g = [part[l, pl.ds(ca * 512 + jk * 8, 8), :] for ca in range(9)]
             target[n, pl.ds(jk * 8, 8), :] = middle_eigen([g[0:3], g[3:6], g[6:9]])
-            return carry
-
-        lax.fori_loop(0, 64, point_row, 0, unroll=16)
 
     for l in range(layers):
         if l in (0, last):
@@ -289,8 +317,8 @@
 
 
 def outer_kernel(last, devices, capacity, *refs):
-    (rx, ry, rz, lam_ends, lo_first, hi_last, inner), hbm, send_hbm = refs[:7], refs[7:13], refs[13]
-    local, (lam, along, store, send, sems) = refs[14:20], refs[20:]
+    (rx, ry, rz, lam_ends, lo_first, hi_last, inner), hbm, send = refs[:7], refs[7:13], refs[13]
+    local, (lam, along, store, sems) = refs[14:20], refs[20:]
     waits = started(list(zip(hbm, local)), sems)
     lam[...] = lam_ends[...]
     for copy in waits:
@@ -305,7 +333,6 @@
     total = send.shape[0]
     parts = 4 if total % 32 == 0 else 1
     size = total // parts
-    outs = []
     for n in range(parts):
         rows = iota((size, CROSS), 0) + n * size
 
@@ -315,36 +342,25 @@
         homes = iota((size, devices), 1) * (capacity + 1) + capacity
         numbered = onehot(iota((size, devices), 0) + n * size == homes)
         both = dot_nt(chosen(range(1, last)), inner[...]) + dot_nt(chosen((0, last)), store[...]) + dot(numbered, numbers)
-        at = pl.ds(n * size, size)
-        send[at, :] = both[:, :128] + both[:, 128:]
-        copy = pltpu.make_async_copy(send.at[at], send_hbm.at[at], sems.at[6 + n])
-        copy.start()
-        outs.append(copy)
-    for copy in outs:
-        copy.wait()
+        send[pl.ds(n * size, size), :] = both[:, :128] + both[:, 128:]
 
 
 def gather_kernel(devices, capacity, rows_ref, out_hbm, halves, ids, image, sems):
-    total = devices * (capacity + 1)
-    wide = halves.shape[0]
-    high, low = halves_of(rows_ref[...])
-    halves[:total, :128] = high
-    halves[:total, 128:] = low
-    if wide > total:
-        halves[total:, :] = jnp.zeros((wide - total, 256), BF16)
+    total = devices * capacity
+    for n in range(devices):
+        high, low = halves_of(rows_ref[pl.ds(n * (capacity + 1), capacity), :])
+        halves[pl.ds(n * capacity, capacity), :] = jnp.concatenate([high, low], axis=1)
     numbers = rows_ref[pl.ds(capacity, devices, stride=capacity + 1), :]
-    column = iota((128, wide), 1)
-    spread = onehot(iota((128, wide), 0) == column % (capacity + 1))
+    spread = onehot(iota((128, total), 0) == iota((128, total), 1) % capacity)
     high, low = halves_of(numbers)
     tiled = dot(high, spread) + dot(low, spread)
-    at = iota((devices, wide), 1)
-    mine = (at // (capacity + 1) == iota((devices, wide), 0)) & (at % (capacity + 1) < capacity)
+    mine = iota((devices, total), 1) // capacity == iota((devices, total), 0)
     found = jnp.sum(jnp.where(mine, tiled + 1.0, 0.0), axis=0, keepdims=True) - 1.0
     ids[...] = found.astype(jnp.int32)
     step = 256
     outs = []
     for n in range(BLOCKS // step):
-        named = onehot(iota((step, wide), 0) + n * step == ids[...])
+        named = onehot(iota((step, total), 0) + n * step == ids[...])
         both = dot(named, halves[...])
         at = pl.ds(n * step, step)
         image[at, :] = both[:, :128] + both[:, 128:]
@@ -384,7 +400,7 @@
     last = elements // CROSS - 1
     devices = lax.axis_size("dom")
     capacity = max(2, 4 * elements // devices)
-    whole, faces = (jnp.asarray(o) for o in operators())
+    across, blocks = (jnp.asarray(o) for o in operator_rows())
     layers = last + 1
     face = (576, CROSS)
     face_shape = jax.ShapeDtypeStruct(face, F32)
@@ -394,10 +410,10 @@
         functools.partial(rim_kernel, last),
         "rim_faces",
         3,
-        in_specs=[NEAR] * 3,
+        in_specs=[NEAR] * 2,
         out_specs=[NEAR] * 2,
         out_shape=[face_shape] * 2,
-    )(faces, velocity, inverse_sizes)
+    )(velocity, inverse_sizes)
     from_prev = lax.ppermute(rim_hi, "dom", [(i, (i + 1) % devices) for i in range(devices)])
     from_next = lax.ppermute(rim_lo, "dom", [((i + 1) % devices, i) for i in range(devices)])
 
@@ -406,8 +422,8 @@
     inner, lam_ends, lo_first, hi_last = kernel_call(
         functools.partial(inner_kernel, layers),
         "inner_layers",
-        9,
-        in_specs=[NEAR] * 6,
+        8,
+        in_specs=[NEAR] * 7,
         out_specs=[NEAR] * 4,
         out_shape=[jax.ShapeDtypeStruct((256, (layers - 2) * 256), BF16), ends_shape, face_shape, face_shape],
         scratch_shapes=[
@@ -415,7 +431,7 @@
             pltpu.VMEM((1, 512, CROSS), F32),
             along,
         ],
-    )(whole, velocity, inverse_sizes, *weights)
+    )(across, blocks, velocity, inverse_sizes, *weights)
 
     rows = devices * (capacity + 1)
     routing = (
@@ -429,7 +445,7 @@
         "outer_layers",
         5,
         in_specs=[NEAR] * 7 + [FAR] * 6,
-        out_specs=FAR,
+        out_specs=NEAR,
         out_shape=jax.ShapeDtypeStruct((rows, 128), F32),
         scratch_shapes=[pltpu.VMEM(face, F32)] * 2
         + [pltpu.VMEM(array.shape, array.dtype) for array in routing]
@@ -437,15 +453,13 @@
             pltpu.VMEM(ends_shape.shape, F32),
             along,
             pltpu.VMEM((256, 512), BF16),
-            pltpu.VMEM((rows, 128), F32),
-            pltpu.SemaphoreType.DMA((10,)),
+            pltpu.SemaphoreType.DMA((6,)),
         ],
     )(*weights, lam_ends, lo_first, hi_last, inner, from_prev, from_next, *routing)
 
     received = lax.all_to_all(
         sendbuf.reshape(devices, 1, (capacity + 1) * 128), "dom", split_axis=0, concat_axis=0, tiled=True
     )
-    wide = -(-rows // 128) * 128
     image = kernel_call(
         functools.partial(gather_kernel, devices, capacity),
         "block_sums",
@@ -454,8 +468,8 @@
         out_specs=FAR,
         out_shape=jax.ShapeDtypeStruct((BLOCKS, 128), F32),
         scratch_shapes=[
-            pltpu.VMEM((wide, 256), BF16),
-            pltpu.VMEM((1, wide), jnp.int32),
+            pltpu.VMEM((devices * capacity, 256), BF16),
+            pltpu.VMEM((1, devices * capacity), jnp.int32),
             pltpu.VMEM((BLOCKS, 128), F32),
             pltpu.SemaphoreType.DMA((8,)),
         ],

time: 58.5 us -> 55.3 us (0.945)
  Pallas kernels: 17.7 us -> 14.6 us
  local copies, waits for them, and re-layouts: 3.14 us -> 2.15 us
  blocking collectives: 30.8 us -> 31.7 us
    pallas_call x1, Pallas kernels: 5.07 us -> 3.09 us  [shards(): kernel_call(functools.partial(outer_kernel, last, devices, capacity), 'ou...]
    pallas_call x1, Pallas kernels: 7.91 us -> 6.52 us  [shards(): kernel_call(functools.partial(inner_kernel, layers), 'inner_layers', 8, i...]
    unnamed x24, local copies, waits for them, and re-layouts: 3.14 us -> 2.15 us
    all_to_all x1, blocking collectives: 30.8 us -> 31.7 us  [shards(): lax.all_to_all(sendbuf.reshape(devices, 1, (capacity + 1) * 128), 'dom',...]
    pallas_call x1, Pallas kernels: 0.97 us -> 1.7 us  [shards(): kernel_call(functools.partial(rim_kernel, last), 'rim_faces', 3, in_specs...]
  transfers between devices with their start and end apart: 2 -> 2, of which waited for: 0 -> 0; matrix products, arithmetic and copies ran while one was open for 0% -> 0% of each run, Pallas kernels for 14% -> 12%
where the time goes in v4:
time: 55.3 us; the launch traced here: 55.1 us
  blocking collectives  31.7 us (57%)
  Pallas kernels  14.6 us (26%)
  starting transfers between devices  6.53 us (12%)
  local copies, waits for them, and re-layouts  2.15 us (4%)
    all_to_all x1, blocking collectives, shards(): lax.all_to_all(sendbuf.reshape(devices, 1, (capacity + 1) * 128), 'dom',...  31.7 us
    pallas_call x1, Pallas kernels, shards(): kernel_call(functools.partial(inner_kernel, layers), 'inner_layers', 8, i...  6.52 us
    ppermute x1, starting transfers between devices, shards(): lax.ppermute(rim_lo, 'dom', [((i + 1) % devices, i) for i in range(device...  6.02 us
    pallas_call x1, Pallas kernels, shards(): kernel_call(functools.partial(gather_kernel, devices, capacity), 'block_s...  3.32 us
    pallas_call x1, Pallas kernels, shards(): kernel_call(functools.partial(outer_kernel, last, devices, capacity), 'ou...  3.09 us
    unnamed x24, local copies, waits for them, and re-layouts  2.15 us
    pallas_call x1, Pallas kernels, shards(): kernel_call(functools.partial(rim_kernel, last), 'rim_faces', 3, in_specs...  1.7 us
  transfers between devices with their start and end apart: 2, of which 0 were waited for; matrix products, arithmetic and copies ran while one was open for 0% of the time, Pallas kernels for 12%

profile of v4, /device:TPU:0, one launch (start us, length us, event | category | flops | bytes accessed | tf_op | source)
XLA Modules:
  0.0 55.1 jit_solution(8046112977652256155)
XLA Ops:
  0.0 0.0 copy-start
  0.0 1.4 %copy-done = bf16[3,512,512]{2,1,0:T(8,128)(2,1)S(1)} copy-done((bf16[3,512,512]{2,1,0:T(8,128)(2,1)S(1)}, bf16[3,512,512]{2,1,0:T(8,128)(2,1)}, u32[]{:S(2)}) %copy-start) | copy-done | bytes 1572888
  1.4 0.0 copy-start.5
  1.4 0.7 %copy-done.5 = f32[3,512]{1,0:T(4,128)S(1)} copy-done((f32[3,512]{1,0:T(4,128)S(1)}, f32[3,512]{1,0:T(4,128)}, u32[]{:S(2)}) %copy-start.5) | copy-done | bytes 6168
  2.1 0.0 copy-start.1
  2.1 0.0 copy-start.2
  2.1 0.0 copy-start.3
  2.1 0.0 copy-start.4
  2.1 0.0 copy-start.10
  2.1 0.0 copy-start.11
  2.1 1.7 %rim_faces.1 = (f32[576,128]{1,0:T(8,128)S(1)}, f32[576,128]{1,0:T(8,128)S(1)}) custom-call(bf16[3,512,512]{2,1,0:T(8,128)(2,1)S(1)} %copy-done, f32[3,512]{1,0:T(4,128)S(1)} %copy-done.5), custom_call_target="tpu_custom_call" | custom-call | flops 3000000000 | tf_op jit(solution)/shard_map/rim_faces/pallas_call | solution.py:409
  3.8 0.5 collective-permute-start
  4.4 0.0 copy-start.6
  4.4 0.0 copy-start.7
  4.4 0.0 copy-start.8
  4.4 6.0 %collective-permute-start.1 = (f32[576,128]{1,0:T(8,128)S(1)}, f32[576,128]{1,0:T(8,128)S(1)}, u32[]{:S(2)}, u32[]{:S(2)}) collective-permute-start(f32[576,128]{1,0:T(8,128)S(1)} %get-tuple-element.16), channel_id=1, source_target_pairs={{1,0},{2,1},{3,2},{4,3},{5,4},{6,5},{7,6},{8,7},{9,8},{10,9},{11,1... | collective-permute-start | bytes 884744 | tf_op jit(solution)/shard_map/ppermute | solution.py:418
  10.4 0.0 copy-done.1
  10.4 0.0 copy-done.2
  10.4 0.0 copy-done.3
  10.4 0.0 copy-done.4
  10.4 0.0 copy-done.10
  10.4 0.0 copy-done.11
  10.4 6.5 %inner_layers.1 = (bf16[256,512]{1,0:T(8,128)(2,1)S(1)}, f32[2,512,128]{2,1,0:T(8,128)S(1)}, f32[576,128]{1,0:T(8,128)S(1)}, f32[576,128]{1,0:T(8,128)S(1)}) custom-call(bf16[512,512]{1,0:T(8,128)(2,1)S(1)} %copy-done.11, bf16[2,2,256,256]{3,2,1,0:T(8,128)(2,1)S(1)} %copy-done.10, bf16[3,512,512]{2,1,0:T(8,128)(2,1)S(1)} %copy-done.1, ...), custom_call_target="tpu_custom_call" | custom-call | flops 8000000000 | tf_op jit(solution)/shard_map/inner_layers/pallas_call | solution.py:422
  16.9 0.0 collective-permute-done.refs_7_
  17.0 0.0 collective-permute-done.1.refs_8_
  17.0 0.0 copy-done.6
  17.0 0.0 copy-done.7
  17.0 0.0 copy-done.8
  17.0 0.0 copy-done.9
  17.0 3.1 %outer_layers.1 = f32[2080,128]{1,0:T(8,128)S(1)} custom-call(f32[2,8,8,512]{3,2,1,0:T(8,128)S(1)} %copy-done.2, f32[2,4,8,512]{3,2,1,0:T(8,128)S(1)} %copy-done.3, f32[2,4,8,512]{3,2,1,0:T(8,128)S(1)} %copy-done.4, f32[2,512,128]{2,1,0:T(8,128)S(1)} %get-tuple-element.11.refs_3_, f32[576,128]{1,0:T(8,128)S(1)} %get-tuple-element.12.refs_4_, ...), custom_call_target="tpu_custom_call" | custom-call | flops 5000000000 | tf_op jit(solution)/shard_map/outer_layers/pallas_call | solution.py:443
  20.1 31.7 %all_to_all.5 = f32[32,1,8320]{2,1,0:T(1,128)S(1)} all-to-all(f32[32,1,8320]{2,1,0:T(1,128)S(1)} %bitcast.6), channel_id=1, replica_groups=mesh['dom'=32] {'dom'}, dimensions={0} | all-to-all | bytes 2129920 | tf_op jit(solution)/shard_map/all_to_all | solution.py:460
  51.8 3.3 %block_sums.1 = f32[2048,128]{1,0:T(8,128)} custom-call(f32[2080,128]{1,0:T(8,128)S(1)} %bitcast.7), custom_call_target="tpu_custom_call" | custom-call | flops 4000000000 | tf_op jit(solution)/shard_map/block_sums/pallas_call | solution.py:463
  (1 shorter events, 0.0 us)
Async XLA Ops:
  0.0 1.4 %copy-start = (bf16[3,512,512]{2,1,0:T(8,128)(2,1)S(1)}, bf16[3,512,512]{2,1,0:T(8,128)(2,1)}, u32[]{:S(2)}) copy-start(bf16[3,512,512]{2,1,0:T(8,128)(2,1)} %vel.3) | copy-start | bytes 4718596
  1.4 0.7 %copy-start.5 = (f32[3,512]{1,0:T(4,128)S(1)}, f32[3,512]{1,0:T(4,128)}, u32[]{:S(2)}) copy-start(f32[3,512]{1,0:T(4,128)} %sizes.3) | copy-start | bytes 18436
  2.1 8.3 %copy-start.1 = (bf16[3,512,512]{2,1,0:T(8,128)(2,1)S(1)}, bf16[3,512,512]{2,1,0:T(8,128)(2,1)}, u32[]{:S(2)}) copy-start(bf16[3,512,512]{2,1,0:T(8,128)(2,1)} %vel.3) | copy-start | bytes 4718596
  2.1 8.3 %copy-start.2 = (f32[2,8,8,512]{3,2,1,0:T(8,128)S(1)}, f32[2,8,8,512]{3,2,1,0:T(8,128)}, u32[]{:S(2)}) copy-start(f32[2,8,8,512]{3,2,1,0:T(8,128)} %refs_0_.1) | copy-start | bytes 786436
  2.1 8.3 %copy-start.3 = (f32[2,4,8,512]{3,2,1,0:T(8,128)S(1)}, f32[2,4,8,512]{3,2,1,0:T(8,128)}, u32[]{:S(2)}) copy-start(f32[2,4,8,512]{3,2,1,0:T(8,128)} %refs_1_.1) | copy-start | bytes 393220
  2.1 8.3 %copy-start.4 = (f32[2,4,8,512]{3,2,1,0:T(8,128)S(1)}, f32[2,4,8,512]{3,2,1,0:T(8,128)}, u32[]{:S(2)}) copy-start(f32[2,4,8,512]{3,2,1,0:T(8,128)} %refs_2_.1) | copy-start | bytes 393220
  2.1 8.3 %copy-start.10 = (bf16[2,2,256,256]{3,2,1,0:T(8,128)(2,1)S(1)}, bf16[2,2,256,256]{3,2,1,0:T(8,128)(2,1)}, u32[]{:S(2)}) copy-start(bf16[2,2,256,256]{3,2,1,0:T(8,128)(2,1)} %constant.5.clone.blocks) | copy-start | bytes 1572868
  2.1 8.3 %copy-start.11 = (bf16[512,512]{1,0:T(8,128)(2,1)S(1)}, bf16[512,512]{1,0:T(8,128)(2,1)}, u32[]{:S(2)}) copy-start(bf16[512,512]{1,0:T(8,128)(2,1)} %constant.4.clone.across) | copy-start | bytes 1572868
  3.8 13.1 %collective-permute-start = (f32[576,128]{1,0:T(8,128)S(1)}, f32[576,128]{1,0:T(8,128)S(1)}, u32[]{:S(2)}, u32[]{:S(2)}) collective-permute-start(f32[576,128]{1,0:T(8,128)S(1)} %get-tuple-element.15), channel_id=1, source_target_pairs={{0,1},{1,2},{2,3},{3,4},{4,5},{5,6},{6,7},{7,8},{8,9},{9,10},{10,1... | collective-permute-start | bytes 884744 | tf_op jit(solution)/shard_map/ppermute | solution.py:417
  4.4 12.6 %copy-start.6 = (s32[2,512]{1,0:T(2,128)S(1)}, s32[2,512]{1,0:T(2,128)}, u32[]{:S(2)}) copy-start(s32[2,512]{1,0:T(2,128)} %refs_9_.1) | copy-start | bytes 12292
  4.4 12.6 %copy-start.7 = (s32[512,1]{0,1:T(1,128)S(1)}, s32[512,1]{0,1:T(1,128)}, u32[]{:S(2)}) copy-start(s32[512,1]{0,1:T(1,128)} %param.17) | copy-start | bytes 6148
  4.4 12.6 %copy-start.8 = (s32[512]{0:T(512)S(1)}, s32[512]{0:T(512)}, u32[]{:S(2)}) copy-start(s32[512]{0:T(512)} %param.18) | copy-start | bytes 6148
  4.4 12.6 %copy-start.9 = (s32[32]{0:T(128)S(1)}, s32[32]{0:T(128)}, u32[]{:S(2)}) copy-start(s32[32]{0:T(128)} %param.19) | copy-start | bytes 388
  4.4 12.6 %collective-permute-start.1 = (f32[576,128]{1,0:T(8,128)S(1)}, f32[576,128]{1,0:T(8,128)S(1)}, u32[]{:S(2)}, u32[]{:S(2)}) collective-permute-start(f32[576,128]{1,0:T(8,128)S(1)} %get-tuple-element.16), channel_id=1, source_target_pairs={{1,0},{2,1},{3,2},{4,3},{5,4},{6,5},{7,6},{8,7},{9,8},{10,9},{11,1... | collective-permute-start | bytes 884744 | tf_op jit(solution)/shard_map/ppermute | solution.py:418
